TPU v7x, 32 devices: a whole 2x2x4 slice. The times are simulated.
32 devices in a mesh: dp: 8 (over y, x, core), seq: 4 (over z).
Axes of the slice: x: 2, y: 2, z: 4, core: 2. Of those that a mesh axis runs over, the one named last changes fastest.
Arguments:
- enc_input: bfloat16 [32, 1024, 512], P('dp', 'seq'), may hold values from -6 to 6
- dec_input: bfloat16 [32, 100, 512], P('dp', 'seq'), may hold values from -6 to 6
- targets: float32 [32, 100, 14], P('dp', 'seq'), may hold values from -6 to 6
- lengths: int32 [32], P('dp'), may hold values from 1 to 100, as said below
- attention_mats: float32 [12, 512, 512], P(None, ('dp', 'seq')), may hold values from -1.8856181 to 1.8856181
- expand_mats: float32 [2, 512, 3200], P(None, ('dp', 'seq')), may hold values from -0.25 to 0.25
- reduce_mats: float32 [2, 3200, 512], P(None, None, ('dp', 'seq')), may hold values from -0.109375 to 0.109375
- action_head: float32 [512, 14], P(('dp', 'seq')), may hold values from -0.25 to 0.25
- query_pos: float32 [100, 512], P(None, ('dp', 'seq')), may hold values from -3 to 3
- vectors: float32 [21, 512], P(None, ('dp', 'seq')), may hold values from -1.2 to 1.4, as said below
- expand_bias: float32 [6400], P(('dp', 'seq')), may hold values from -1 to 1
- first_attention: float32 [12, 512, 512], P(None, ('dp', 'seq')), may hold values from -0.875 to 0.875
- first_expand: float32 [2, 512, 3200], P(None, ('dp', 'seq')), may hold values from -0.875 to 0.875
- first_reduce: float32 [2, 3200, 512], P(None, None, ('dp', 'seq')), may hold values from -0.875 to 0.875
- first_head: float32 [512, 14], P(('dp', 'seq')), may hold values from -3.5 to 3.5
- first_query: float32 [100, 512], P(None, ('dp', 'seq')), may hold values from -0.01953125 to 0.01953125
- first_vectors: float32 [21, 512], P(None, ('dp', 'seq')), may hold values from -1.75 to 1.75
- first_bias: float32 [6400], P(('dp', 'seq')), may hold values from -0.4375 to 0.4375
- second_attention: float32 [12, 512, 512], P(None, ('dp', 'seq')), may hold values from 0.00016 to 0.00256
- second_expand: float32 [2, 512, 3200], P(None, ('dp', 'seq')), may hold values from 0.00016 to 0.00256
- second_reduce: float32 [2, 3200, 512], P(None, None, ('dp', 'seq')), may hold values from 0.00016 to 0.00256
- second_head: float32 [512, 14], P(('dp', 'seq')), may hold values from 0.00256 to 0.04096
- second_query: float32 [100, 512], P(None, ('dp', 'seq')), may hold values from 6.4e-08 to 1.024e-06
- second_vectors: float32 [21, 512], P(None, ('dp', 'seq')), may hold values from 0.00064 to 0.01024
- second_bias: float32 [6400], P(('dp', 'seq')), may hold values from 4e-05 to 0.00064
Outputs:
- enc_input_grad: bfloat16 [32, 1024, 512], P('dp', 'seq')
- dec_input_grad: bfloat16 [32, 100, 512], P('dp', 'seq')
- first_attention_new: float32 [12, 512, 512], P(None, ('dp', 'seq'))
- second_attention_new: float32 [12, 512, 512], P(None, ('dp', 'seq'))
- attention_master: float32 [12, 512, 512], P(None, ('dp', 'seq'))
- attention_half: bfloat16 [12, 512, 512], P(None, ('dp', 'seq'))
- first_expand_new: float32 [2, 512, 3200], P(None, ('dp', 'seq'))
- second_expand_new: float32 [2, 512, 3200], P(None, ('dp', 'seq'))
- expand_master: float32 [2, 512, 3200], P(None, ('dp', 'seq'))
- expand_half: bfloat16 [2, 512, 3200], P(None, ('dp', 'seq'))
- first_reduce_new: float32 [2, 3200, 512], P(None, None, ('dp', 'seq'))
- second_reduce_new: float32 [2, 3200, 512], P(None, None, ('dp', 'seq'))
- reduce_master: float32 [2, 3200, 512], P(None, None, ('dp', 'seq'))
- reduce_half: bfloat16 [2, 3200, 512], P(None, None, ('dp', 'seq'))
- first_head_new: float32 [512, 14], P(('dp', 'seq'))
- second_head_new: float32 [512, 14], P(('dp', 'seq'))
- head_master: float32 [512, 14], P(('dp', 'seq'))
- head_half: bfloat16 [512, 14], P(('dp', 'seq'))
- first_query_new: float32 [100, 512], P(None, ('dp', 'seq'))
- second_query_new: float32 [100, 512], P(None, ('dp', 'seq'))
- query_master: float32 [100, 512], P(None, ('dp', 'seq'))
- query_half: bfloat16 [100, 512], P(None, ('dp', 'seq'))
- first_vectors_new: float32 [21, 512], P(None, ('dp', 'seq'))
- second_vectors_new: float32 [21, 512], P(None, ('dp', 'seq'))
- vectors_master: float32 [21, 512], P(None, ('dp', 'seq'))
- vectors_half: bfloat16 [21, 512], P(None, ('dp', 'seq'))
- first_bias_new: float32 [6400], P(('dp', 'seq'))
- second_bias_new: float32 [6400], P(('dp', 'seq'))
- bias_master: float32 [6400], P(('dp', 'seq'))
- bias_half: bfloat16 [6400], P(('dp', 'seq'))
Inputs may be any that keep to these rules, and one draw needn't show every extreme that they name: `lengths`: in each aligned group of 4 items one item has all 100 steps valid. `vectors`: rows 3, 6, 11, 16 and 19 are LayerNorm gains, the other rows biases and shifts.
All inputs are finite; a program needn't handle non-finite values.
Results may differ from a plain program's by a relative error of at most 0.02.
Values may be sent and summed in bfloat16 or wider, within the bound.
No kernel may reach another device: no remote copies, remote signals or barrier semaphores. Data moves between devices by JAX's collectives and lax.ppermute only.
A program may use at most 256 MiB of HBM per device.

v0:
```python
import math

import jax
import jax.numpy as jnp
from jax import lax
from jax.sharding import PartitionSpec as P

HEADS = 8
HDIM = 64
STEP = 10


beta_first = 0.9
beta_second = 0.999
epsilon = 1e-08
decay_rate = 0.1
rate_matrix = 0.08
rate_vector = 0.2


def to_half(values):
    return values.astype(jnp.bfloat16)


def project(inputs, weight):
    return jnp.einsum("brk,kn->brn", inputs, weight, preferred_element_type=jnp.float32)


def project_back(gradient, weight):
    return jnp.einsum("brn,kn->brk", gradient, weight, preferred_element_type=jnp.float32)


def outer_sum(inputs, gradient):
    return jnp.einsum("brk,brn->kn", inputs, gradient, preferred_element_type=jnp.float32)


def column_sum(values):
    return jnp.sum(values.astype(jnp.float32), axis=(0, 1))


def layer_norm(values, gain, shift):
    center = values - jnp.mean(values, axis=-1, keepdims=True)
    spread = jnp.mean(center * center, axis=-1, keepdims=True)
    return center * lax.rsqrt(spread + 1e-05) * gain + shift


def norm_back(values, gain, shift, gradient):
    unused_out, pullback = jax.vjp(layer_norm, values, gain, shift)
    return pullback(gradient)


def gelu_back(inner, gradient):
    unused_out, pullback = jax.vjp(jax.nn.gelu, inner)
    return pullback(gradient)[0]


def sine_table(places, width):
    halves = jnp.arange(width // 2).astype(jnp.float32)
    frequency = jnp.exp(halves * (-2.0 * math.log(10000.0) / width))
    angles = places[:, None] * frequency[None, :]
    return jnp.stack([jnp.sin(angles), jnp.cos(angles)], axis=-1).reshape(places.shape[0], width)


def split_heads(values):
    return values.reshape(values.shape[0], values.shape[1], HEADS, HDIM)


def by_groups(function, arrays):
    count = arrays[0].shape[0]
    group = 2
    grouped = tuple((array.reshape((count // group, group) + array.shape[1:]) for array in arrays))
    result = lax.map(lambda pieces: function(*pieces), grouped)
    return jax.tree.map(lambda array: array.reshape((count,) + array.shape[2:]), result)


def attend(query, keys, values):
    query_heads = split_heads(query)
    key_heads = split_heads(keys)
    value_heads = split_heads(values)
    raw = jnp.einsum("bqhd,bkhd->bhqk", query_heads, key_heads, preferred_element_type=jnp.float32)
    scores = raw * HDIM ** (-0.5)
    peak = jnp.max(scores, axis=-1, keepdims=True)
    log_total = peak + jnp.log(jnp.sum(jnp.exp(scores - peak), axis=-1, keepdims=True))
    probs = to_half(jnp.exp(scores - log_total))
    mixed = jnp.einsum("bhqk,bkhd->bqhd", probs, value_heads, preferred_element_type=jnp.float32)
    return (mixed.reshape(query.shape), log_total)


def score_parts(query, keys, values, log_total, out_grad):
    query_heads = split_heads(query)
    key_heads = split_heads(keys)
    value_heads = split_heads(values)
    grad_heads = split_heads(out_grad)
    raw = jnp.einsum("bqhd,bkhd->bhqk", query_heads, key_heads, preferred_element_type=jnp.float32)
    probs = jnp.exp(raw * HDIM ** (-0.5) - log_total)
    prob_grad = jnp.einsum(
        "bqhd,bkhd->bhqk", grad_heads, value_heads, preferred_element_type=jnp.float32
    )
    weighted = jnp.sum(probs * prob_grad, axis=-1, keepdims=True)
    score_grad = to_half(probs * (prob_grad - weighted) * HDIM ** (-0.5))
    return (query_heads, key_heads, grad_heads, probs, score_grad, weighted)


def attend_query_back(query, keys, values, log_total, out_grad):
    query_heads, key_heads, grad_heads, probs, score_grad, weighted = score_parts(
        query, keys, values, log_total, out_grad
    )
    query_grad = jnp.einsum(
        "bhqk,bkhd->bqhd", score_grad, key_heads, preferred_element_type=jnp.float32
    )
    return (query_grad.reshape(query.shape), weighted)


def key_side(query, keys, values, log_total, weighted, out_grad):
    query_heads = split_heads(query)
    key_heads = split_heads(keys)
    value_heads = split_heads(values)
    grad_heads = split_heads(out_grad)
    raw = jnp.einsum("bqhd,bkhd->bhqk", query_heads, key_heads, preferred_element_type=jnp.float32)
    probs = jnp.exp(raw * HDIM ** (-0.5) - log_total)
    value_grad = jnp.einsum(
        "bhqk,bqhd->bkhd", to_half(probs), grad_heads, preferred_element_type=jnp.float32
    )
    prob_grad = jnp.einsum(
        "bqhd,bkhd->bhqk", grad_heads, value_heads, preferred_element_type=jnp.float32
    )
    score_grad = to_half(probs * (prob_grad - weighted) * HDIM ** (-0.5))
    key_grad = jnp.einsum(
        "bhqk,bqhd->bkhd", score_grad, query_heads, preferred_element_type=jnp.float32
    )
    return (key_grad.reshape(keys.shape), value_grad.reshape(values.shape))


def adamw(weight, gradient, moment_one, moment_two, step_rate):
    moment_one = beta_first * moment_one + (1.0 - beta_first) * gradient
    moment_two = beta_second * moment_two + (1.0 - beta_second) * gradient * gradient
    mean_hat = moment_one / (1.0 - beta_first**STEP)
    square_hat = moment_two / (1.0 - beta_second**STEP)
    updated = weight - step_rate * (
        mean_hat / (jnp.sqrt(square_hat) + epsilon) + decay_rate * weight
    )
    return (moment_one, moment_two, updated, updated.astype(jnp.bfloat16))


def per_device(
    enc_input,
    dec_input,
    targets,
    lengths,
    attention_mats,
    expand_mats,
    reduce_mats,
    action_head,
    query_pos,
    vectors,
    expand_bias,
    first_attention,
    first_expand,
    first_reduce,
    first_head,
    first_query,
    first_vectors,
    first_bias,
    second_attention,
    second_expand,
    second_reduce,
    second_head,
    second_query,
    second_vectors,
    second_bias,
):
    seq_index = lax.axis_index("seq")
    enc_rows = enc_input.shape[1]
    dec_rows = dec_input.shape[1]
    positions = sine_table(
        (seq_index * enc_rows + jnp.arange(enc_rows)).astype(jnp.float32), enc_input.shape[2]
    )
    enc_local = (
        to_half(attention_mats[0:4]),
        to_half(expand_mats[0]),
        to_half(reduce_mats[0]),
        to_half(vectors[0:8]),
        to_half(expand_bias),
    )
    enc_mats, enc_expand, enc_reduce, enc_vec_half, bias_half = (
        lax.all_gather(enc_local[0], ("dp", "seq"), axis=1, tiled=True),
        lax.all_gather(enc_local[1], ("dp", "seq"), axis=0, tiled=True),
        lax.all_gather(enc_local[2], ("dp", "seq"), axis=1, tiled=True),
        lax.all_gather(enc_local[3], ("dp", "seq"), axis=1, tiled=True),
        lax.all_gather(enc_local[4], ("dp", "seq"), axis=0, tiled=True),
    )
    enc_vec = enc_vec_half.astype(jnp.float32)
    bias_all = bias_half.astype(jnp.float32)
    width_ff = enc_expand.shape[1]
    enc_float = enc_input.astype(jnp.float32)
    enc_in_half = to_half(enc_float + positions)
    enc_query = to_half(project(enc_in_half, enc_mats[0]) + enc_vec[0])
    enc_keys = to_half(project(enc_in_half, enc_mats[1]))
    enc_values = to_half(project(enc_input, enc_mats[2]) + enc_vec[1])
    keys_all, values_all = (
        lax.all_gather(enc_keys, "seq", axis=1, tiled=True),
        lax.all_gather(enc_values, "seq", axis=1, tiled=True),
    )
    enc_mixed, enc_log_total = by_groups(attend, (enc_query, keys_all, values_all))
    enc_mixed_half = to_half(enc_mixed)
    enc_sum_one = enc_float + project(enc_mixed_half, enc_mats[3]) + enc_vec[2]
    enc_hidden = layer_norm(enc_sum_one, enc_vec[3], enc_vec[4])
    enc_hidden_half = to_half(enc_hidden)
    enc_inner = project(enc_hidden_half, enc_expand) + bias_all[:width_ff]
    enc_act_half = to_half(jax.nn.gelu(enc_inner))
    enc_sum_two = enc_hidden + project(enc_act_half, enc_reduce) + enc_vec[5]
    memory = layer_norm(enc_sum_two, enc_vec[6], enc_vec[7])
    dec_local = (
        to_half(attention_mats[4:12]),
        to_half(expand_mats[1]),
        to_half(reduce_mats[1]),
        to_half(action_head),
        to_half(query_pos),
        to_half(vectors[8:21]),
    )
    dec_mats, dec_expand, dec_reduce, head_whole, query_whole, dec_vec_half = (
        lax.all_gather(dec_local[0], ("dp", "seq"), axis=1, tiled=True),
        lax.all_gather(dec_local[1], ("dp", "seq"), axis=0, tiled=True),
        lax.all_gather(dec_local[2], ("dp", "seq"), axis=1, tiled=True),
        lax.all_gather(dec_local[3], ("dp", "seq"), axis=0, tiled=True),
        lax.all_gather(dec_local[4], ("dp", "seq"), axis=1, tiled=True),
        lax.all_gather(dec_local[5], ("dp", "seq"), axis=1, tiled=True),
    )
    dec_vec = dec_vec_half.astype(jnp.float32)
    dec_float = dec_input.astype(jnp.float32)
    pos_rows = lax.dynamic_slice_in_dim(query_whole, seq_index * dec_rows, dec_rows, 0).astype(
        jnp.float32
    )
    self_in = to_half(dec_float + pos_rows)
    self_query = to_half(project(self_in, dec_mats[0]) + dec_vec[0])
    self_keys = to_half(project(self_in, dec_mats[1]))
    self_values = to_half(project(dec_input, dec_mats[2]) + dec_vec[1])
    memory_in = to_half(memory + positions)
    memory_half = to_half(memory)
    cross_keys = to_half(project(memory_in, dec_mats[5]))
    cross_values = to_half(project(memory_half, dec_mats[6]) + dec_vec[6])
    self_keys_all, self_values_all, cross_keys_all, cross_values_all = (
        lax.all_gather(self_keys, "seq", axis=1, tiled=True),
        lax.all_gather(self_values, "seq", axis=1, tiled=True),
        lax.all_gather(cross_keys, "seq", axis=1, tiled=True),
        lax.all_gather(cross_values, "seq", axis=1, tiled=True),
    )
    self_mixed, self_log = by_groups(attend, (self_query, self_keys_all, self_values_all))
    self_mixed_half = to_half(self_mixed)
    dec_sum_one = dec_float + project(self_mixed_half, dec_mats[3]) + dec_vec[2]
    dec_one = layer_norm(dec_sum_one, dec_vec[3], dec_vec[4])
    cross_in = to_half(dec_one + pos_rows)
    cross_query = to_half(project(cross_in, dec_mats[4]) + dec_vec[5])
    cross_mixed, cross_log = by_groups(attend, (cross_query, cross_keys_all, cross_values_all))
    cross_mixed_half = to_half(cross_mixed)
    dec_sum_two = dec_one + project(cross_mixed_half, dec_mats[7]) + dec_vec[7]
    dec_two = layer_norm(dec_sum_two, dec_vec[8], dec_vec[9])
    dec_two_half = to_half(dec_two)
    dec_inner = project(dec_two_half, dec_expand) + bias_all[width_ff:]
    dec_act_half = to_half(jax.nn.gelu(dec_inner))
    dec_sum_three = dec_two + project(dec_act_half, dec_reduce) + dec_vec[10]
    dec_three = layer_norm(dec_sum_three, dec_vec[11], dec_vec[12])
    dec_three_half = to_half(dec_three)
    predicted = project(dec_three_half, head_whole)
    step_index = seq_index * dec_rows + jnp.arange(dec_rows)
    valid = (step_index[None, :] < lengths[:, None]).astype(jnp.float32)
    error = predicted - targets
    pred_grad = to_half(error * lax.rsqrt(error * error + 1.0) * valid[:, :, None] / error.shape[2])
    back_mats, back_expand, back_reduce, back_head, back_vec_half = (
        lax.all_gather(dec_local[0], ("dp", "seq"), axis=1, tiled=True),
        lax.all_gather(dec_local[1], ("dp", "seq"), axis=0, tiled=True),
        lax.all_gather(dec_local[2], ("dp", "seq"), axis=1, tiled=True),
        lax.all_gather(dec_local[3], ("dp", "seq"), axis=0, tiled=True),
        lax.all_gather(dec_local[5], ("dp", "seq"), axis=1, tiled=True),
    )
    back_vec = back_vec_half.astype(jnp.float32)
    head_grad = outer_sum(dec_three_half, pred_grad)
    three_grad = project_back(pred_grad, back_head)
    sum_three_grad, gain_three, shift_three = norm_back(
        dec_sum_three, back_vec[11], back_vec[12], three_grad
    )
    reduce_out_half = to_half(sum_three_grad)
    dec_reduce_grad = outer_sum(dec_act_half, reduce_out_half)
    dec_act_grad = project_back(reduce_out_half, back_reduce)
    dec_inner_half = to_half(gelu_back(dec_inner, dec_act_grad))
    dec_expand_grad = outer_sum(dec_two_half, dec_inner_half)
    two_grad = sum_three_grad + project_back(dec_inner_half, back_expand)
    sum_two_grad, gain_two, shift_two = norm_back(dec_sum_two, back_vec[8], back_vec[9], two_grad)
    cross_out_half = to_half(sum_two_grad)
    cross_out_wgrad = outer_sum(cross_mixed_half, cross_out_half)
    cross_mixed_grad = to_half(project_back(cross_out_half, back_mats[7]))
    cross_query_grad, cross_weighted = by_groups(
        attend_query_back,
        (cross_query, cross_keys_all, cross_values_all, cross_log, cross_mixed_grad),
    )
    cross_query_half = to_half(cross_query_grad)
    cross_query_wgrad = outer_sum(cross_in, cross_query_half)
    cross_in_grad = project_back(cross_query_half, back_mats[4])
    one_grad = sum_two_grad + cross_in_grad
    sum_one_grad, gain_one, shift_one = norm_back(dec_sum_one, back_vec[3], back_vec[4], one_grad)
    self_out_half = to_half(sum_one_grad)
    self_out_wgrad = outer_sum(self_mixed_half, self_out_half)
    self_mixed_grad = to_half(project_back(self_out_half, back_mats[3]))
    self_query_grad, self_weighted = by_groups(
        attend_query_back, (self_query, self_keys_all, self_values_all, self_log, self_mixed_grad)
    )
    self_query_all, self_grad_all, cross_query_all, cross_grad_all = (
        lax.all_gather(self_query, "seq", axis=1, tiled=True),
        lax.all_gather(self_mixed_grad, "seq", axis=1, tiled=True),
        lax.all_gather(cross_query, "seq", axis=1, tiled=True),
        lax.all_gather(cross_mixed_grad, "seq", axis=1, tiled=True),
    )
    self_log_all, self_weighted_all, cross_log_all, cross_weighted_all = (
        lax.all_gather(self_log, "seq", axis=2, tiled=True),
        lax.all_gather(self_weighted, "seq", axis=2, tiled=True),
        lax.all_gather(cross_log, "seq", axis=2, tiled=True),
        lax.all_gather(cross_weighted, "seq", axis=2, tiled=True),
    )
    self_key_grad, self_value_grad = by_groups(
        key_side,
        (self_query_all, self_keys, self_values, self_log_all, self_weighted_all, self_grad_all),
    )
    cross_key_grad, cross_value_grad = by_groups(
        key_side,
        (
            cross_query_all,
            cross_keys,
            cross_values,
            cross_log_all,
            cross_weighted_all,
            cross_grad_all,
        ),
    )
    self_query_half = to_half(self_query_grad)
    self_key_half = to_half(self_key_grad)
    self_value_half = to_half(self_value_grad)
    cross_key_half = to_half(cross_key_grad)
    cross_value_half = to_half(cross_value_grad)
    self_in_grad = project_back(self_query_half, back_mats[0]) + project_back(
        self_key_half, back_mats[1]
    )
    dec_input_grad = to_half(
        sum_one_grad + self_in_grad + project_back(self_value_half, back_mats[2])
    )
    pos_grad_rows = jnp.sum(self_in_grad + cross_in_grad, axis=0)
    pos_grad = lax.dynamic_update_slice_in_dim(
        jnp.zeros((dec_rows * lax.axis_size("seq"), pos_grad_rows.shape[1]), jnp.float32),
        pos_grad_rows,
        seq_index * dec_rows,
        0,
    )
    memory_grad = project_back(cross_key_half, back_mats[5]) + project_back(
        cross_value_half, back_mats[6]
    )
    dec_mat_grads = jnp.stack(
        [
            outer_sum(self_in, self_query_half),
            outer_sum(self_in, self_key_half),
            outer_sum(dec_input, self_value_half),
            self_out_wgrad,
            cross_query_wgrad,
            outer_sum(memory_in, cross_key_half),
            outer_sum(memory_half, cross_value_half),
            cross_out_wgrad,
        ]
    )
    dec_vec_grads = jnp.stack(
        [
            column_sum(self_query_half),
            column_sum(self_value_half),
            column_sum(sum_one_grad),
            gain_one,
            shift_one,
            column_sum(cross_query_half),
            column_sum(cross_value_half),
            column_sum(sum_two_grad),
            gain_two,
            shift_two,
            column_sum(sum_three_grad),
            gain_three,
            shift_three,
        ]
    )
    dec_bias_grad = column_sum(dec_inner_half)
    dec_sums = (
        lax.psum_scatter(dec_mat_grads, ("dp", "seq"), scatter_dimension=1, tiled=True),
        lax.psum_scatter(dec_expand_grad, ("dp", "seq"), scatter_dimension=0, tiled=True),
        lax.psum_scatter(dec_reduce_grad, ("dp", "seq"), scatter_dimension=1, tiled=True),
        lax.psum_scatter(head_grad, ("dp", "seq"), scatter_dimension=0, tiled=True),
        lax.psum_scatter(pos_grad, ("dp", "seq"), scatter_dimension=1, tiled=True),
        lax.psum_scatter(dec_vec_grads, ("dp", "seq"), scatter_dimension=1, tiled=True),
    )
    enc_back_mats, enc_back_expand, enc_back_reduce, enc_back_half = (
        lax.all_gather(enc_local[0], ("dp", "seq"), axis=1, tiled=True),
        lax.all_gather(enc_local[1], ("dp", "seq"), axis=0, tiled=True),
        lax.all_gather(enc_local[2], ("dp", "seq"), axis=1, tiled=True),
        lax.all_gather(enc_local[3], ("dp", "seq"), axis=1, tiled=True),
    )
    enc_back_vec = enc_back_half.astype(jnp.float32)
    enc_two_grad, enc_gain_two, enc_shift_two = norm_back(
        enc_sum_two, enc_back_vec[6], enc_back_vec[7], memory_grad
    )
    enc_out_half = to_half(enc_two_grad)
    enc_reduce_grad = outer_sum(enc_act_half, enc_out_half)
    enc_act_grad = project_back(enc_out_half, enc_back_reduce)
    enc_inner_half = to_half(gelu_back(enc_inner, enc_act_grad))
    enc_expand_grad = outer_sum(enc_hidden_half, enc_inner_half)
    hidden_grad = enc_two_grad + project_back(enc_inner_half, enc_back_expand)
    enc_one_grad, enc_gain_one, enc_shift_one = norm_back(
        enc_sum_one, enc_back_vec[3], enc_back_vec[4], hidden_grad
    )
    attn_out_half = to_half(enc_one_grad)
    enc_out_wgrad = outer_sum(enc_mixed_half, attn_out_half)
    enc_mixed_grad = to_half(project_back(attn_out_half, enc_back_mats[3]))
    enc_query_grad, enc_weighted = by_groups(
        attend_query_back, (enc_query, keys_all, values_all, enc_log_total, enc_mixed_grad)
    )
    enc_query_all, enc_grad_all = (
        lax.all_gather(enc_query, "seq", axis=1, tiled=True),
        lax.all_gather(enc_mixed_grad, "seq", axis=1, tiled=True),
    )
    enc_log_all, enc_weighted_all = (
        lax.all_gather(enc_log_total.astype(jnp.bfloat16), "seq", axis=2, tiled=True).astype(
            enc_log_total.dtype
        ),
        lax.all_gather(enc_weighted.astype(jnp.bfloat16), "seq", axis=2, tiled=True).astype(
            enc_weighted.dtype
        ),
    )
    enc_key_grad, enc_value_grad = by_groups(
        key_side, (enc_query_all, enc_keys, enc_values, enc_log_all, enc_weighted_all, enc_grad_all)
    )
    enc_query_half = to_half(enc_query_grad)
    enc_key_half = to_half(enc_key_grad)
    enc_value_half = to_half(enc_value_grad)
    enc_input_grad = to_half(
        enc_one_grad
        + project_back(enc_query_half, enc_back_mats[0])
        + project_back(enc_key_half, enc_back_mats[1])
        + project_back(enc_value_half, enc_back_mats[2])
    )
    enc_mat_grads = jnp.stack(
        [
            outer_sum(enc_in_half, enc_query_half),
            outer_sum(enc_in_half, enc_key_half),
            outer_sum(enc_input, enc_value_half),
            enc_out_wgrad,
        ]
    )
    enc_vec_grads = jnp.stack(
        [
            column_sum(enc_query_half),
            column_sum(enc_value_half),
            column_sum(enc_one_grad),
            enc_gain_one,
            enc_shift_one,
            column_sum(enc_two_grad),
            enc_gain_two,
            enc_shift_two,
        ]
    )
    bias_grads = jnp.concatenate([column_sum(enc_inner_half), dec_bias_grad])
    enc_sums = (
        lax.psum_scatter(enc_mat_grads, ("dp", "seq"), scatter_dimension=1, tiled=True),
        lax.psum_scatter(enc_expand_grad, ("dp", "seq"), scatter_dimension=0, tiled=True),
        lax.psum_scatter(enc_reduce_grad, ("dp", "seq"), scatter_dimension=1, tiled=True),
        lax.psum_scatter(enc_vec_grads, ("dp", "seq"), scatter_dimension=1, tiled=True),
        lax.psum_scatter(bias_grads, ("dp", "seq"), scatter_dimension=0, tiled=True),
    )
    gradients = (
        jnp.concatenate([enc_sums[0], dec_sums[0]], axis=0),
        jnp.stack([enc_sums[1], dec_sums[1]]),
        jnp.stack([enc_sums[2], dec_sums[2]]),
        dec_sums[3],
        dec_sums[4],
        jnp.concatenate([enc_sums[3], dec_sums[5]], axis=0),
        enc_sums[4],
    )
    weights = (
        attention_mats,
        expand_mats,
        reduce_mats,
        action_head,
        query_pos,
        vectors,
        expand_bias,
    )
    firsts = (
        first_attention,
        first_expand,
        first_reduce,
        first_head,
        first_query,
        first_vectors,
        first_bias,
    )
    seconds = (
        second_attention,
        second_expand,
        second_reduce,
        second_head,
        second_query,
        second_vectors,
        second_bias,
    )
    rates = (
        rate_matrix,
        rate_matrix,
        rate_matrix,
        rate_matrix,
        rate_vector,
        rate_vector,
        rate_vector,
    )
    outputs = [enc_input_grad, dec_input_grad]
    for weight, gradient, moment_one, moment_two, step_rate in zip(
        weights, gradients, firsts, seconds, rates
    ):
        outputs.extend(adamw(weight, gradient, moment_one, moment_two, step_rate))
    return tuple(outputs)


def solution(mesh):
    in_specs = (
        P("dp", "seq", None),
        P("dp", "seq", None),
        P("dp", "seq", None),
        P("dp"),
        P(None, ("dp", "seq"), None),
        P(None, ("dp", "seq"), None),
        P(None, None, ("dp", "seq")),
        P(("dp", "seq"), None),
        P(None, ("dp", "seq")),
        P(None, ("dp", "seq")),
        P(("dp", "seq")),
        P(None, ("dp", "seq"), None),
        P(None, ("dp", "seq"), None),
        P(None, None, ("dp", "seq")),
        P(("dp", "seq"), None),
        P(None, ("dp", "seq")),
        P(None, ("dp", "seq")),
        P(("dp", "seq")),
        P(None, ("dp", "seq"), None),
        P(None, ("dp", "seq"), None),
        P(None, None, ("dp", "seq")),
        P(("dp", "seq"), None),
        P(None, ("dp", "seq")),
        P(None, ("dp", "seq")),
        P(("dp", "seq")),
    )
    out_specs = (
        P("dp", "seq", None),
        P("dp", "seq", None),
        P(None, ("dp", "seq"), None),
        P(None, ("dp", "seq"), None),
        P(None, ("dp", "seq"), None),
        P(None, ("dp", "seq"), None),
        P(None, ("dp", "seq"), None),
        P(None, ("dp", "seq"), None),
        P(None, ("dp", "seq"), None),
        P(None, ("dp", "seq"), None),
        P(None, None, ("dp", "seq")),
        P(None, None, ("dp", "seq")),
        P(None, None, ("dp", "seq")),
        P(None, None, ("dp", "seq")),
        P(("dp", "seq"), None),
        P(("dp", "seq"), None),
        P(("dp", "seq"), None),
        P(("dp", "seq"), None),
        P(None, ("dp", "seq")),
        P(None, ("dp", "seq")),
        P(None, ("dp", "seq")),
        P(None, ("dp", "seq")),
        P(None, ("dp", "seq")),
        P(None, ("dp", "seq")),
        P(None, ("dp", "seq")),
        P(None, ("dp", "seq")),
        P(("dp", "seq")),
        P(("dp", "seq")),
        P(("dp", "seq")),
        P(("dp", "seq")),
    )
    return jax.shard_map(
        per_device, mesh=mesh, in_specs=in_specs, out_specs=out_specs, check_vma=False
    )
```

profile of v0, /device:TPU:0, one launch (start us, length us, event | category | flops | bytes accessed | tf_op | source)
XLA Modules:
  0.0 2517.3 jit_solution(8891534639130984893)
XLA Ops:
  9.8 70.3 %all-gather.4 = bf16[32,16,8]{1,2,0:T(8,128)(2,1)S(1)} all-gather(bf16[1,16,8]{1,2,0:T(8,128)(2,1)S(1)} %slice_bitcast_fusion.36), channel_id=1, replica_groups=mesh['dp'=8,'seq'=4] {'dp','seq'}, dimensions={0}, use_global_device_ids=true | all-gather | bytes 8448 | tf_op jit(solution)/shard_map/all_gather | solution.py:189
  91.7 41.2 %all-reduce = bf16[6400]{0:T(1024)(128)(2,1)S(1)} all-reduce(bf16[6400]{0:T(1024)(128)(2,1)S(1)} %dynamic-update-slice), channel_id=1, replica_groups=mesh['dp'=8,'seq'=4] {'dp','seq'}, use_global_device_ids=true, to_apply=%add | all-reduce | flops 6400 | bytes 25600
  133.5 70.4 %all_gather.97 = bf16[13,512]{0,1:T(8,128)(2,1)S(1)} all-gather(bf16[13,16]{0,1:T(8,128)(2,1)S(1)} %copy.663), channel_id=1, replica_groups=mesh['dp'=8,'seq'=4] {'dp','seq'}, dimensions={1}, use_global_device_ids=true | all-gather | bytes 13728 | tf_op jit(solution)/shard_map/all_gather | solution.py:227
  215.5 29.1 %all-gather.24.cloned.1.call-done = bf16[4,1024,512]{2,1,0:T(8,128)(2,1)} async-done(((bf16[4,256,512]{2,1,0:T(8,128)(2,1)}), bf16[4,1024,512]{2,1,0:T(8,128)(2,1)}) %all-gather.24.cloned.1.call-update) | async-done | bytes 4194320 | tf_op jit(solution)/shard_map/all_gather | solution.py:201
  251.0 25.5 %while.109 = (s32[]{:T(128)}, bf16[2,2,256,512]{2,3,1,0:T(8,128)(2,1)S(1)}, f32[2,2,8,256,1]{3,2,1,4,0:T(8,128)S(1)}, bf16[2,2,1024,512]{2,3,1,0:T(8,128)(2,1)},...) while((s32[]{:T(128)}, bf16[2,2,256,512]{2,3,1,0:T(8,128)(2,1)S(1)}, ...), condition=%wide.region_9.10_spmd, body=%wide.region_6.9_spmd.sunk | while | flops 1107292160 | bytes 66191460 | solution.py:72
  280.6 25.3 %all-gather.34.cloned.1.call-done = bf16[1,512,3200]{2,1,0:T(8,128)(2,1)} async-done(((bf16[1,16,3200]{2,1,0:T(8,128)(2,1)}), bf16[1,512,3200]{2,1,0:T(8,128)(2,1)}) %all-gather.34.cloned.1.call-update) | async-done | bytes 3276816 | tf_op jit(solution)/shard_map/all_gather | solution.py:187
  314.6 52.8 %all-gather.36.cloned.1.call-done = bf16[1,3200,512]{1,2,0:T(8,128)(2,1)} async-done(((bf16[1,3200,16]{1,2,0:T(8,128)(2,1)}), bf16[1,3200,512]{1,2,0:T(8,128)(2,1)}) %all-gather.36.cloned.1.call-update) | async-done | bytes 3276816 | tf_op jit(solution)/shard_map/all_gather | solution.py:188
  378.1 53.6 %all-gather.18.cloned.1.call-done = bf16[8,512,512]{2,1,0:T(8,128)(2,1)} async-done(((bf16[8,16,512]{2,1,0:T(8,128)(2,1)}), bf16[8,512,512]{2,1,0:T(8,128)(2,1)}) %all-gather.18.cloned.1.call-update) | async-done | bytes 4194320 | tf_op jit(solution)/shard_map/all_gather | solution.py:222
  438.9 69.4 %all_gather.99 = bf16[100,512]{0,1:T(8,128)(2,1)S(1)} all-gather(bf16[100,16]{0,1:T(8,128)(2,1)S(1)} %convert_element_type.376), channel_id=1, replica_groups=mesh['dp'=8,'seq'=4] {'dp','seq'}, dimensions={1}, use_global_device_ids=true | all-gather | bytes 105600 | tf_op jit(solution)/shard_map/all_gather | solution.py:226
  508.6 71.5 %all_gather.114 = bf16[512,14]{1,0:T(8,128)(2,1)} all-gather(bf16[16,14]{1,0:T(8,128)(2,1)S(1)} %convert_element_type.412), channel_id=1, replica_groups=mesh['dp'=8,'seq'=4] {'dp','seq'}, dimensions={0}, use_global_device_ids=true | all-gather | bytes 14784 | tf_op jit(solution)/shard_map/all_gather | solution.py:225
  586.5 18.6 all_gather.100
  605.6 14.9 all_gather.98
  623.9 14.8 all_gather.122
  642.7 17.0 all_gather.101
  772.5 17.2 all_gather.111
  790.0 15.2 all_gather.116
  805.3 18.1 all_gather.115
  825.9 15.1 while.112
  857.5 14.5 all_gather.123
  890.4 14.6 convert_reduce_fusion
  916.1 74.3 %while.113 = (s32[]{:T(128)}, bf16[2,2,256,512]{2,3,1,0:T(8,128)(2,1)}, bf16[2,2,8,256,1]{3,2,1,4,0:T(8,128)(2,1)S(1)}, bf16[2,2,1024,512]{2,3,1,0:T(8,128)(2,1)...) while((s32[]{:T(128)}, ...), condition=%wide.region_37.38_spmd, body=%wide.region_35.37_spmd.sunk | while | flops 1652551680 | bytes 188350704 | solution.py:72
  1017.3 87.4 %while.114 = (s32[]{:T(128)}, bf16[2,2,256,512]{2,3,1,0:T(8,128)(2,1)}, bf16[2,2,256,512]{2,3,1,0:T(8,128)(2,1)}, bf16[2,2,1024,512]{3,2,1,0:T(8,128)(2,1)}, bf1...) while((s32[]{:T(128)}, ...), condition=%wide.region_39.40_spmd, body=%wide.region_38.39_spmd.sunk | while | flops 2185232384 | bytes 101122288 | solution.py:72
  1168.7 39.9 %all-reduce.1 = f32[6400]{0:T(1024)S(1)} all-reduce(f32[6400]{0:T(1024)S(1)} %pad_maximum_fusion.4), channel_id=16, replica_groups=mesh['dp'=8,'seq'=4] {'dp','seq'}, use_global_device_ids=true, to_apply=%region_81.82.clone | all-reduce | flops 6400 | bytes 51200
  1214.0 50.3 %reduce-scatter.29.cloned.1.call-done = f32[100,16]{0,1:T(8,128)} async-done(((f32[100,512]{0,1:T(8,128)}), f32[100,16]{0,1:T(8,128)}) %reduce-scatter.29.cloned.1.call-update) | async-done | bytes 6416 | tf_op jit(solution)/shard_map/reduce_scatter | solution.py:390
  1271.1 126.0 %reduce-scatter.33.cloned.1.call-done = f32[16,13]{1,0:T(8,128)} async-done(((f32[512,13]{1,0:T(8,128)}), f32[16,13]{1,0:T(8,128)}) %reduce-scatter.33.cloned.1.call-update) | async-done | bytes 848
  1397.1 132.3 %reduce-scatter.31.cloned.1.call-done = f32[16,8]{1,0:T(8,128)} async-done(((f32[512,8]{1,0:T(8,128)}), f32[16,8]{1,0:T(8,128)}) %reduce-scatter.31.cloned.1.call-update) | async-done | bytes 528
  1530.9 156.6 %reduce-scatter.23.cloned.1.call-done = f32[3200,16]{0,1:T(8,128)} async-done(((f32[3200,512]{0,1:T(8,128)}), f32[3200,16]{0,1:T(8,128)}) %reduce-scatter.23.cloned.1.call-update) | async-done | bytes 204816 | tf_op jit(solution)/shard_map/reduce_scatter | solution.py:466
  1687.5 162.2 %reduce-scatter.25.cloned.1.call-done = f32[3200,16]{0,1:T(8,128)} async-done(((f32[3200,512]{0,1:T(8,128)}), f32[3200,16]{0,1:T(8,128)}) %reduce-scatter.25.cloned.1.call-update) | async-done | bytes 204816 | tf_op jit(solution)/shard_map/reduce_scatter | solution.py:388
  1852.3 158.4 %reduce-scatter.19.cloned.1.call-done = f32[16,3200]{1,0:T(8,128)} async-done(((f32[512,3200]{1,0:T(8,128)}), f32[16,3200]{1,0:T(8,128)}) %reduce-scatter.19.cloned.1.call-update) | async-done | bytes 204816 | tf_op jit(solution)/shard_map/reduce_scatter | solution.py:465
  2010.7 161.0 %reduce-scatter.21.cloned.1.call-done = f32[16,3200]{1,0:T(8,128)} async-done(((f32[512,3200]{1,0:T(8,128)}), f32[16,3200]{1,0:T(8,128)}) %reduce-scatter.21.cloned.1.call-update) | async-done | bytes 204816 | tf_op jit(solution)/shard_map/reduce_scatter | solution.py:387
  2174.0 147.6 %reduce-scatter.15.cloned.1.call-done = f32[4,16,512]{2,1,0:T(8,128)} async-done(((f32[4,512,512]{2,1,0:T(8,128)}), f32[4,16,512]{2,1,0:T(8,128)}) %reduce-scatter.15.cloned.1.call-update) | async-done | bytes 131088 | tf_op jit(solution)/shard_map/reduce_scatter | solution.py:464
  2322.5 185.5 %reduce-scatter.17.cloned.1.call-done = f32[8,16,512]{2,1,0:T(8,128)} async-done(((f32[8,512,512]{2,1,0:T(8,128)}), f32[8,16,512]{2,1,0:T(8,128)}) %reduce-scatter.17.cloned.1.call-update) | async-done | bytes 262160 | tf_op jit(solution)/shard_map/reduce_scatter | solution.py:386
  (874 shorter events, 582.9 us)
Async XLA Ops:
  7.2 73.3 %all-gather.20.cloned.1.call-start = ((), (), s32[]{:S(2)}) async-start(), calls=%async_computation.11 | async-start | bytes 2162688 | tf_op jit(solution)/shard_map/all_gather | solution.py:186
  8.9 200.3 %all-gather.22.cloned.1.call-start = ((), (), s32[]{:S(2)}) async-start(), calls=%async_computation.12 | async-start | bytes 5242880 | tf_op jit(solution)/shard_map/all_gather | solution.py:202
  80.4 354.1 %copy-start.142 = (f32[1,512]{1,0:T(1,128)}, f32[1,512]{1,0:T(1,128)S(1)}, u32[]{:S(2)}) copy-start(f32[1,512]{1,0:T(1,128)S(1)} %get-tuple-element.1375) | copy-start | bytes 6148
  83.5 161.2 %all-gather.24.cloned.1.call-start = ((), (), s32[]{:S(2)}) async-start(), calls=%async_computation.13 | async-start | bytes 5242880 | tf_op jit(solution)/shard_map/all_gather | solution.py:201
  88.9 217.0 %all-gather.34.cloned.1.call-start = ((), (), s32[]{:S(2)}) async-start(), calls=%async_computation.26 | async-start | bytes 3379200 | tf_op jit(solution)/shard_map/all_gather | solution.py:187
  89.7 277.7 %all-gather.36.cloned.1.call-start = ((), (), s32[]{:S(2)}) async-start(), calls=%async_computation.27 | async-start | bytes 3379200 | tf_op jit(solution)/shard_map/all_gather | solution.py:188
  90.5 341.1 %all-gather.18.cloned.1.call-start = ((), (), s32[]{:S(2)}) async-start(), calls=%async_computation.10 | async-start | bytes 4325376 | tf_op jit(solution)/shard_map/all_gather | solution.py:222
  91.3 599.1 %all-gather.26.cloned.1.call-start = ((), (), s32[]{:S(2)}) async-start(), calls=%async_computation.14 | async-start | bytes 5242880 | tf_op jit(solution)/shard_map/all_gather | solution.py:246
  276.6 400.0 %copy-start.67 = (f32[2,2,8,256,1]{3,2,1,4,0:T(8,128)}, f32[2,2,8,256,1]{3,2,1,4,0:T(8,128)S(1)}, u32[]{:S(2)}) copy-start(f32[2,2,8,256,1]{3,2,1,4,0:T(8,128)S(1)} %get-tuple-element.2060) | copy-start | bytes 98308
  377.6 510.4 %copy-start.107 = (f32[4,256]{1,0:T(4,128)}, f32[4,256]{1,0:T(4,128)S(1)}, u32[]{:S(2)}) copy-start(f32[4,256]{1,0:T(4,128)S(1)} %broadcast_multiply_fusion) | copy-start | bytes 12292
  434.5 262.3 %all-gather.28.cloned.1.call-start = ((), (), s32[]{:S(2)}) async-start(), calls=%async_computation.15 | async-start | bytes 5242880 | tf_op jit(solution)/shard_map/all_gather | solution.py:245
  437.5 277.6 %all-gather.38.cloned.1.call-start = ((), (), s32[]{:S(2)}) async-start(), calls=%async_computation.28 | async-start | bytes 3379200 | tf_op jit(solution)/shard_map/all_gather | solution.py:223
  438.2 292.8 %all-gather.40.cloned.1.call-start = ((), (), s32[]{:S(2)}) async-start(), calls=%async_computation.29 | async-start | bytes 3379200 | tf_op jit(solution)/shard_map/all_gather | solution.py:224
  438.8 576.4 %all-gather.30.cloned.1.call-start = ((), (), s32[]{:S(2)}) async-start(), calls=%async_computation.16 | async-start | bytes 5242880 | tf_op jit(solution)/shard_map/all_gather | solution.py:419
  581.4 433.8 %all-gather.32.cloned.1.call-start = ((), (), s32[]{:S(2)}) async-start(), calls=%async_computation.17 | async-start | bytes 5242880 | tf_op jit(solution)/shard_map/all_gather | solution.py:420
  915.0 297.5 %reduce-scatter.27.cloned.1.call-start = ((), (), s32[]{:S(2)}) async-start(), calls=%async_computation.24 | async-start | bytes 270336 | tf_op jit(solution)/shard_map/reduce_scatter | solution.py:389
  992.1 272.2 %reduce-scatter.29.cloned.1.call-start = ((), (), s32[]{:S(2)}) async-start(), calls=%async_computation.25 | async-start | bytes 270336 | tf_op jit(solution)/shard_map/reduce_scatter | solution.py:390
  997.7 399.4 %reduce-scatter.33.cloned.1.call-start = ((), (), s32[]{:S(2)}) async-start(), calls=%async_computation.31 | async-start | bytes 270336
  1015.1 514.3 %reduce-scatter.31.cloned.1.call-start = ((), (), s32[]{:S(2)}) async-start(), calls=%async_computation.30 | async-start | bytes 270336
  1107.8 579.7 %reduce-scatter.23.cloned.1.call-start = ((), (), s32[]{:S(2)}) async-start(), calls=%async_computation.22 | async-start | bytes 6758400 | tf_op jit(solution)/shard_map/reduce_scatter | solution.py:466
  1120.1 729.6 %reduce-scatter.25.cloned.1.call-start = ((), (), s32[]{:S(2)}) async-start(), calls=%async_computation.23 | async-start | bytes 6758400 | tf_op jit(solution)/shard_map/reduce_scatter | solution.py:388
  1125.5 885.2 %reduce-scatter.19.cloned.1.call-start = ((), (), s32[]{:S(2)}) async-start(), calls=%async_computation.20 | async-start | bytes 6758400 | tf_op jit(solution)/shard_map/reduce_scatter | solution.py:465
  1135.8 1035.8 %reduce-scatter.21.cloned.1.call-start = ((), (), s32[]{:S(2)}) async-start(), calls=%async_computation.21 | async-start | bytes 6758400 | tf_op jit(solution)/shard_map/reduce_scatter | solution.py:387
  1140.9 1180.7 %reduce-scatter.15.cloned.1.call-start = ((), (), s32[]{:S(2)}) async-start(), calls=%async_computation.18 | async-start | bytes 4325376 | tf_op jit(solution)/shard_map/reduce_scatter | solution.py:464
  1150.0 1358.0 %reduce-scatter.17.cloned.1.call-start = ((), (), s32[]{:S(2)}) async-start(), calls=%async_computation.19 | async-start | bytes 8650752 | tf_op jit(solution)/shard_map/reduce_scatter | solution.py:386
  1267.9 581.8 %copy-start.53 = (f32[2,3200,16]{1,2,0:T(8,128)S(1)}, f32[2,3200,16]{1,2,0:T(8,128)}, u32[]{:S(2)}) copy-start(f32[2,3200,16]{1,2,0:T(8,128)} %param.49) | copy-start | bytes 1228804
  1271.1 900.6 %copy-start.55 = (f32[2,16,3200]{2,1,0:T(8,128)S(1)}, f32[2,16,3200]{2,1,0:T(8,128)}, u32[]{:S(2)}) copy-start(f32[2,16,3200]{2,1,0:T(8,128)} %param.48) | copy-start | bytes 1228804
  1271.1 900.6 %copy-start.77 = (f32[2,16,3200]{2,1,0:T(8,128)S(1)}, f32[2,16,3200]{2,1,0:T(8,128)}, u32[]{:S(2)}) copy-start(f32[2,16,3200]{2,1,0:T(8,128)} %param.62) | copy-start | bytes 1228804
  1271.1 900.6 %copy-start.78 = (f32[2,16,3200]{2,1,0:T(8,128)S(1)}, f32[2,16,3200]{2,1,0:T(8,128)}, u32[]{:S(2)}) copy-start(f32[2,16,3200]{2,1,0:T(8,128)} %param.55) | copy-start | bytes 1228804
  1852.3 656.7 %copy-start.57 = (f32[12,16,512]{2,1,0:T(8,128)S(1)}, f32[12,16,512]{2,1,0:T(8,128)}, u32[]{:S(2)}) copy-start(f32[12,16,512]{2,1,0:T(8,128)} %param.47) | copy-start | bytes 1179652
  1852.3 656.7 %copy-start.79 = (f32[12,16,512]{2,1,0:T(8,128)S(1)}, f32[12,16,512]{2,1,0:T(8,128)}, u32[]{:S(2)}) copy-start(f32[12,16,512]{2,1,0:T(8,128)} %param.61) | copy-start | bytes 1179652
  1852.3 656.7 %copy-start.80 = (f32[12,16,512]{2,1,0:T(8,128)S(1)}, f32[12,16,512]{2,1,0:T(8,128)}, u32[]{:S(2)}) copy-start(f32[12,16,512]{2,1,0:T(8,128)} %param.54) | copy-start | bytes 1179652
  (198 other events, 4375.9 us)
Sparse Core Ops, SparseCore 0:
  11.6 58.9 all-gather.19
  83.7 79.1 all-gather.21
  164.4 80.2 all-gather.23
  247.9 57.9 all-gather.33
  309.2 58.2 all-gather.35
  370.9 60.6 all-gather.17
  434.6 81.5 all-gather.25
  517.8 88.1 all-gather.27
  609.4 58.2 all-gather.37
  670.9 60.1 all-gather.39
  733.2 92.6 all-gather.29
  915.1 80.7 all-gather.31
  998.8 132.4 reduce-scatter.26
  1134.0 130.2 reduce-scatter.28
  1266.9 130.1 reduce-scatter.32
  1399.3 130.1 reduce-scatter.30
  1531.6 155.8 reduce-scatter.22
  1689.6 160.0 reduce-scatter.24
  1852.0 158.6 reduce-scatter.18
  2012.8 158.8 reduce-scatter.20
  2174.0 147.5 reduce-scatter.14
  2323.9 184.1 reduce-scatter.16
where the time goes:
time: 2530 us; the launch traced here: 2520 us
  waiting for transfers between devices  1460 us (58%)
  blocking collectives  548 us (22%)
  matrix products  297 us (12%)
  local copies, waits for them, and re-layouts  152 us (6%)
  other arithmetic  45 us (2%)
    unnamed x24, waiting for transfers between devices  260 us
    reduce_scatter x1, waiting for transfers between devices, per_device(): lax.psum_scatter(dec_mat_grads, ('dp', 'seq'), scatter_dimension=1, tiled...  186 us
    reduce_scatter x1, waiting for transfers between devices, per_device(): lax.psum_scatter(dec_reduce_grad, ('dp', 'seq'), scatter_dimension=1, til...  162 us
    reduce_scatter x1, waiting for transfers between devices, per_device(): lax.psum_scatter(dec_expand_grad, ('dp', 'seq'), scatter_dimension=0, til...  161 us
    reduce_scatter x1, waiting for transfers between devices, per_device(): lax.psum_scatter(enc_expand_grad, ('dp', 'seq'), scatter_dimension=0, til...  158 us
    reduce_scatter x1, waiting for transfers between devices, per_device(): lax.psum_scatter(enc_reduce_grad, ('dp', 'seq'), scatter_dimension=1, til...  157 us
    reduce_scatter x1, waiting for transfers between devices, per_device(): lax.psum_scatter(enc_mat_grads, ('dp', 'seq'), scatter_dimension=1, tiled...  148 us
    unnamed x2, blocking collectives  81.1 us
  transfers between devices with their start and end apart: 22, of which 14 were waited for; matrix products, arithmetic and copies ran while one was open for 18% of the time, Pallas kernels for 0%

commit v1 on v0

v1 whole, which is shorter than its diff:
```python
import functools
import math

import jax
import jax.numpy as jnp
import numpy as np
from jax import lax
from jax.experimental import pallas as pl
from jax.experimental.pallas import tpu as pltpu
from jax.sharding import PartitionSpec as P

HEADS = 8
HDIM = 64
STEP = 10
ALL = ("dp", "seq")

beta_first = 0.9
beta_second = 0.999
epsilon = 1e-08
decay_rate = 0.1
rate_matrix = 0.08
rate_vector = 0.2

BF = jnp.bfloat16
F32 = jnp.float32
MB = 1 << 20


def to_half(values):
    return values.astype(BF)


def mm(a, b):
    return lax.dot_general(a, b, (((1,), (0,)), ((), ())), preferred_element_type=F32)


def mm_t(a, b):
    return lax.dot_general(a, b, (((1,), (1,)), ((), ())), preferred_element_type=F32)


def t_mm(a, b):
    return lax.dot_general(a, b, (((0,), (0,)), ((), ())), preferred_element_type=F32)


def column_sum(values):
    return jnp.sum(values.astype(F32), axis=0)


def layer_norm(values, gain, shift):
    center = values - jnp.mean(values, axis=-1, keepdims=True)
    spread = jnp.mean(center * center, axis=-1, keepdims=True)
    return center * lax.rsqrt(spread + 1e-05) * gain + shift


def norm_back(values, gain, gradient):
    center = values - jnp.mean(values, axis=-1, keepdims=True)
    spread = jnp.mean(center * center, axis=-1, keepdims=True)
    scale = lax.rsqrt(spread + 1e-05)
    unit = center * scale
    inner = gradient * gain
    mean_inner = jnp.mean(inner, axis=-1, keepdims=True)
    mean_cross = jnp.mean(inner * unit, axis=-1, keepdims=True)
    back = scale * (inner - mean_inner - unit * mean_cross)
    return back, jnp.sum(gradient * unit, axis=0), jnp.sum(gradient, axis=0)


def gelu_back(inner, gradient):
    unused_out, pullback = jax.vjp(jax.nn.gelu, inner)
    return pullback(gradient)[0]


def sine_table(count, width):
    halves = np.arange(width // 2, dtype=np.float64)
    frequency = np.exp(halves * (-2.0 * math.log(10000.0) / width))
    angles = np.arange(count)[:, None] * frequency[None, :]
    table = np.stack([np.sin(angles), np.cos(angles)], axis=-1).reshape(count, width)
    return table.astype(np.float32)


def attend_kernel(q_ref, k_ref, v_ref, o_ref, log_ref, *, chunk):
    keys = k_ref[...]
    values_t = v_ref[...].T
    lane = lax.broadcasted_iota(jnp.int32, (chunk, 2 * HDIM), 1)
    row = lax.broadcasted_iota(jnp.int32, (2 * HDIM, chunk), 0)

    def step(i, carry):
        at = pl.ds(i * chunk, chunk)
        query = q_ref[at, :] * BF(HDIM ** (-0.5))
        mixed = []
        for h in range(2):
            own = jnp.where((lane < HDIM) == (h == 0), query, BF(0))
            scores = mm_t(keys, own)
            peak = jnp.max(scores, axis=0, keepdims=True)
            weights = jnp.exp(scores - peak)
            total = jnp.sum(weights, axis=0, keepdims=True)
            mixed.append(mm(values_t, weights.astype(BF)) / total)
            log_ref[0, pl.ds(h, 1), at] = peak + jnp.log(total)
        both = jnp.where(row < HDIM, mixed[0], mixed[1])
        o_ref[at, :] = both.T.astype(BF)
        return carry

    lax.fori_loop(0, q_ref.shape[0] // chunk, step, 0)


def attend(query, keys, values):
    rows, width = query.shape
    pairs = width // (2 * HDIM)
    spec = pl.BlockSpec((rows, 2 * HDIM), lambda i: (0, i))
    return pl.pallas_call(
        functools.partial(attend_kernel, chunk=256),
        grid=(pairs,),
        in_specs=[spec, spec, spec],
        out_specs=[spec, pl.BlockSpec((1, 2, rows), lambda i: (i, 0, 0))],
        out_shape=[
            jax.ShapeDtypeStruct((rows, width), BF),
            jax.ShapeDtypeStruct((pairs, 2, rows), F32),
        ],
        compiler_params=pltpu.CompilerParams(vmem_limit_bytes=48 * MB),
        cost_estimate=pl.CostEstimate(
            flops=16 * rows * rows * width, bytes_accessed=8 * rows * width, transcendentals=rows * rows * 8
        ),
    )(query, keys, values)


def attend_back_kernel(
    q_ref, k_ref, v_ref, o_ref, g_ref, log_ref, dq_ref, dk_ref, dv_ref, dk_acc, dv_acc, *, chunk
):
    keys = k_ref[...]
    keys_t = keys.T
    values = v_ref[...]
    lane = lax.broadcasted_iota(jnp.int32, (chunk, 2 * HDIM), 1)
    row = lax.broadcasted_iota(jnp.int32, (2 * HDIM, chunk), 0)
    scale = HDIM ** (-0.5)
    dk_acc[...] = jnp.zeros_like(dk_acc)
    dv_acc[...] = jnp.zeros_like(dv_acc)

    def step(i, carry):
        at = pl.ds(i * chunk, chunk)
        query = q_ref[at, :] * BF(scale)
        grad = g_ref[at, :]
        cross = (grad.astype(F32) * o_ref[at, :].astype(F32)).T
        query_grads = []
        for h in range(2):
            mine = (lane < HDIM) == (h == 0)
            own = jnp.where(mine, query, BF(0))
            own_grad = jnp.where(mine, grad, BF(0))
            weighted = jnp.sum(cross[h * HDIM : (h + 1) * HDIM], axis=0, keepdims=True)
            probs = jnp.exp(mm_t(keys, own) - log_ref[0, pl.ds(h, 1), at])
            prob_grad = mm_t(values, own_grad)
            score_grad = (probs * (prob_grad - weighted)).astype(BF)
            dv_acc[...] += mm(probs.astype(BF), own_grad)
            dk_acc[...] += mm(score_grad, own)
            query_grads.append(mm(keys_t, score_grad))
        both = jnp.where(row < HDIM, query_grads[0], query_grads[1]) * scale
        dq_ref[at, :] = both.T.astype(BF)
        return carry

    lax.fori_loop(0, q_ref.shape[0] // chunk, step, 0)
    dk_ref[...] = dk_acc[...].astype(BF)
    dv_ref[...] = dv_acc[...].astype(BF)


def attend_back(query, keys, values, mixed, grad, log_total):
    rows, width = query.shape
    pairs = width // (2 * HDIM)
    spec = pl.BlockSpec((rows, 2 * HDIM), lambda i: (0, i))
    return pl.pallas_call(
        functools.partial(attend_back_kernel, chunk=256),
        grid=(pairs,),
        in_specs=[spec] * 5 + [pl.BlockSpec((1, 2, rows), lambda i: (i, 0, 0))],
        out_specs=[spec] * 3,
        out_shape=[jax.ShapeDtypeStruct((rows, width), BF)] * 3,
        scratch_shapes=[pltpu.VMEM((rows, 2 * HDIM), F32)] * 2,
        compiler_params=pltpu.CompilerParams(vmem_limit_bytes=48 * MB),
        cost_estimate=pl.CostEstimate(
            flops=40 * rows * rows * width, bytes_accessed=16 * rows * width, transcendentals=rows * rows * 8
        ),
    )(query, keys, values, mixed, grad, log_total)


def heads_of(values):
    return values.reshape(values.shape[0], HEADS, HDIM)


def small_attend(query, keys, values):
    raw = jnp.einsum("qhd,khd->hqk", heads_of(query), heads_of(keys), preferred_element_type=F32)
    scores = raw * HDIM ** (-0.5)
    peak = jnp.max(scores, axis=-1, keepdims=True)
    weights = jnp.exp(scores - peak)
    probs = weights / jnp.sum(weights, axis=-1, keepdims=True)
    mixed = jnp.einsum("hqk,khd->qhd", to_half(probs), heads_of(values), preferred_element_type=F32)
    return to_half(mixed.reshape(query.shape)), probs


def small_attend_back(query, keys, values, probs, grad):
    prob_grad = jnp.einsum("qhd,khd->hqk", heads_of(grad), heads_of(values), preferred_element_type=F32)
    weighted = jnp.sum(probs * prob_grad, axis=-1, keepdims=True)
    score_grad = to_half(probs * (prob_grad - weighted) * HDIM ** (-0.5))
    dq = jnp.einsum("hqk,khd->qhd", score_grad, heads_of(keys), preferred_element_type=F32)
    dk = jnp.einsum("hqk,qhd->khd", score_grad, heads_of(query), preferred_element_type=F32)
    dv = jnp.einsum("hqk,qhd->khd", to_half(probs), heads_of(grad), preferred_element_type=F32)
    return (
        to_half(dq.reshape(query.shape)),
        to_half(dk.reshape(keys.shape)),
        to_half(dv.reshape(values.shape)),
    )


def adamw(weight, gradient, moment_one, moment_two, step_rate):
    moment_one = beta_first * moment_one + (1.0 - beta_first) * gradient
    moment_two = beta_second * moment_two + (1.0 - beta_second) * gradient * gradient
    mean_hat = moment_one / (1.0 - beta_first**STEP)
    square_hat = moment_two / (1.0 - beta_second**STEP)
    updated = weight - step_rate * (
        mean_hat / (jnp.sqrt(square_hat) + epsilon) + decay_rate * weight
    )
    return (moment_one, moment_two, updated, updated.astype(BF))


def side_by_side(mats):
    return jnp.concatenate([mats[i] for i in range(mats.shape[0])], axis=1)


def pad_rows(values, count):
    return jnp.pad(values, ((0, count - values.shape[0]), (0, 0)))


def pad_columns(values, count):
    return jnp.pad(values, ((0, 0), (0, count - values.shape[1])))


def gather(columns):
    return lax.all_gather(columns, ALL, axis=0, tiled=True)


def scatter(columns):
    return lax.psum_scatter(columns, ALL, scatter_dimension=0, tiled=True).astype(F32)


def per_device(
    enc_input,
    dec_input,
    targets,
    lengths,
    attention_mats,
    expand_mats,
    reduce_mats,
    action_head,
    query_pos,
    vectors,
    expand_bias,
    *moments,
):
    ranks = lax.axis_size("seq")
    seq_index = lax.axis_index("seq")
    items, enc_part, width = enc_input.shape
    dec_part = dec_input.shape[1]
    joints = targets.shape[2]
    width_ff = expand_mats.shape[2]
    shard = attention_mats.shape[1]
    bias_part = expand_bias.shape[0]
    n_query, n_vec = query_pos.shape[0], vectors.shape[0]
    vec_at = (n_query + 7) // 8 * 8
    head_at = (vec_at + n_vec + 7) // 8 * 8
    n_small = (head_at + joints + 127) // 128 * 128
    devices = width // shard

    def pack_small(query, vector, head):
        return pad_columns(
            jnp.concatenate(
                [pad_columns(query, vec_at), pad_columns(vector, head_at - vec_at), head], axis=1
            ),
            n_small,
        )

    half_mats = to_half(attention_mats)
    half_expand = to_half(expand_mats)
    half_reduce = to_half(jnp.swapaxes(reduce_mats, 1, 2))
    small_local = to_half(pack_small(query_pos.T, vectors.T, action_head))
    bias_local = to_half(jnp.pad(expand_bias, (0, shard * 128 - bias_part)).reshape(shard, 128))
    enc_all = gather(
        jnp.concatenate(
            [side_by_side(half_mats[0:4]), half_expand[0], half_reduce[0], small_local, bias_local],
            axis=1,
        )
    )
    dec_all = gather(
        jnp.concatenate([side_by_side(half_mats[4:12]), half_expand[1], half_reduce[1]], axis=1)
    )

    per_rank = items // ranks
    def to_item(values):
        return lax.all_to_all(values, "seq", 0, 1, tiled=True)

    enc_items = to_item(enc_input)
    dec_items = to_item(dec_input)
    target_items = to_item(targets)
    enc_x = enc_items[0]
    dec_x = dec_items[0]
    target = target_items[0]
    length = lengths[seq_index]
    enc_rows = enc_x.shape[0]
    dec_rows = dec_x.shape[0]

    enc_mats = [enc_all[:, i * width : (i + 1) * width] for i in range(4)]
    at = 4 * width
    enc_expand = enc_all[:, at : at + width_ff]
    enc_reduce_t = enc_all[:, at + width_ff : at + 2 * width_ff]
    at += 2 * width_ff
    small = enc_all[:, at : at + n_small].T
    bias_all = (
        enc_all[:, at + n_small :].reshape(devices, shard * 128)[:, :bias_part].reshape(-1).astype(F32)
    )
    query_whole = small[:n_query].astype(F32)
    vec = small[vec_at : vec_at + n_vec].astype(F32)
    head_t = small[head_at : head_at + joints]
    dec_mats = [None] * 4 + [dec_all[:, i * width : (i + 1) * width] for i in range(8)]
    at = 8 * width
    dec_expand = dec_all[:, at : at + width_ff]
    dec_reduce_t = dec_all[:, at + width_ff : at + 2 * width_ff]

    positions = jnp.asarray(sine_table(enc_rows, width))
    enc_float = enc_x.astype(F32)
    enc_in = to_half(enc_float + positions)
    enc_query = to_half(mm(enc_in, enc_mats[0]) + vec[0])
    enc_keys = to_half(mm(enc_in, enc_mats[1]))
    enc_values = to_half(mm(enc_x, enc_mats[2]) + vec[1])
    enc_mixed, enc_log = attend(enc_query, enc_keys, enc_values)
    enc_sum_one = enc_float + mm(enc_mixed, enc_mats[3]) + vec[2]
    enc_hidden = layer_norm(enc_sum_one, vec[3], vec[4])
    enc_hidden_half = to_half(enc_hidden)
    enc_inner = mm(enc_hidden_half, enc_expand) + bias_all[:width_ff]
    enc_act = to_half(jax.nn.gelu(enc_inner))
    enc_sum_two = enc_hidden + mm_t(enc_act, enc_reduce_t) + vec[5]
    memory = layer_norm(enc_sum_two, vec[6], vec[7])

    dec_float = dec_x.astype(F32)
    self_in = to_half(dec_float + query_whole)
    self_query = to_half(mm(self_in, dec_mats[4]) + vec[8])
    self_keys = to_half(mm(self_in, dec_mats[5]))
    self_values = to_half(mm(dec_x, dec_mats[6]) + vec[9])
    self_mixed, self_probs = small_attend(self_query, self_keys, self_values)
    dec_sum_one = dec_float + mm(self_mixed, dec_mats[7]) + vec[10]
    dec_one = layer_norm(dec_sum_one, vec[11], vec[12])
    cross_in = to_half(dec_one + query_whole)
    cross_query = to_half(mm(cross_in, dec_mats[8]) + vec[13])
    memory_in = to_half(memory + positions)
    memory_half = to_half(memory)
    cross_keys = to_half(mm(memory_in, dec_mats[9]))
    cross_values = to_half(mm(memory_half, dec_mats[10]) + vec[14])
    cross_mixed, cross_probs = small_attend(cross_query, cross_keys, cross_values)
    dec_sum_two = dec_one + mm(cross_mixed, dec_mats[11]) + vec[15]
    dec_two = layer_norm(dec_sum_two, vec[16], vec[17])
    dec_two_half = to_half(dec_two)
    dec_inner = mm(dec_two_half, dec_expand) + bias_all[width_ff:]
    dec_act = to_half(jax.nn.gelu(dec_inner))
    dec_sum_three = dec_two + mm_t(dec_act, dec_reduce_t) + vec[18]
    dec_three = layer_norm(dec_sum_three, vec[19], vec[20])
    dec_three_half = to_half(dec_three)
    predicted = mm_t(dec_three_half, head_t)

    valid = (jnp.arange(dec_rows) < length).astype(F32)
    error = predicted - target
    pred_grad = to_half(error * lax.rsqrt(error * error + 1.0) * valid[:, None] / joints)
    head_grad_t = t_mm(pred_grad, dec_three_half)
    three_grad = mm(pred_grad, head_t)
    sum_three_grad, gain_three, shift_three = norm_back(dec_sum_three, vec[19], three_grad)
    reduce_out = to_half(sum_three_grad)
    dec_reduce_grad_t = t_mm(reduce_out, dec_act)
    dec_inner_half = to_half(gelu_back(dec_inner, mm(reduce_out, dec_reduce_t)))
    dec_expand_grad = t_mm(dec_two_half, dec_inner_half)
    two_grad = sum_three_grad + mm_t(dec_inner_half, dec_expand)
    sum_two_grad, gain_two, shift_two = norm_back(dec_sum_two, vec[16], two_grad)
    cross_out = to_half(sum_two_grad)
    cross_out_wgrad = t_mm(cross_mixed, cross_out)
    cross_mixed_grad = to_half(mm_t(cross_out, dec_mats[11]))
    cross_dq, cross_dk, cross_dv = small_attend_back(
        cross_query, cross_keys, cross_values, cross_probs, cross_mixed_grad
    )
    cross_in_grad = mm_t(cross_dq, dec_mats[8])
    one_grad = sum_two_grad + cross_in_grad
    sum_one_grad, gain_one, shift_one = norm_back(dec_sum_one, vec[11], one_grad)
    self_out = to_half(sum_one_grad)
    self_out_wgrad = t_mm(self_mixed, self_out)
    self_mixed_grad = to_half(mm_t(self_out, dec_mats[7]))
    self_dq, self_dk, self_dv = small_attend_back(
        self_query, self_keys, self_values, self_probs, self_mixed_grad
    )
    self_in_grad = mm_t(self_dq, dec_mats[4]) + mm_t(self_dk, dec_mats[5])
    dec_input_grad = to_half(sum_one_grad + self_in_grad + mm_t(self_dv, dec_mats[6]))
    query_grad = self_in_grad + cross_in_grad
    memory_grad = mm_t(cross_dk, dec_mats[9]) + mm_t(cross_dv, dec_mats[10])
    dec_sums = scatter(
        jnp.concatenate(
            [
                to_half(g)
                for g in (
                    t_mm(self_in, self_dq),
                    t_mm(self_in, self_dk),
                    t_mm(dec_x, self_dv),
                    self_out_wgrad,
                    t_mm(cross_in, cross_dq),
                    t_mm(memory_in, cross_dk),
                    t_mm(memory_half, cross_dv),
                    cross_out_wgrad,
                    dec_expand_grad,
                    dec_reduce_grad_t,
                )
            ],
            axis=1,
        )
    )

    enc_two_grad, enc_gain_two, enc_shift_two = norm_back(enc_sum_two, vec[6], memory_grad)
    enc_out = to_half(enc_two_grad)
    enc_reduce_grad_t = t_mm(enc_out, enc_act)
    enc_inner_half = to_half(gelu_back(enc_inner, mm(enc_out, enc_reduce_t)))
    enc_expand_grad = t_mm(enc_hidden_half, enc_inner_half)
    hidden_grad = enc_two_grad + mm_t(enc_inner_half, enc_expand)
    enc_one_grad, enc_gain_one, enc_shift_one = norm_back(enc_sum_one, vec[3], hidden_grad)
    attn_out = to_half(enc_one_grad)
    enc_out_wgrad = t_mm(enc_mixed, attn_out)
    enc_mixed_grad = to_half(mm_t(attn_out, enc_mats[3]))
    enc_dq, enc_dk, enc_dv = attend_back(
        enc_query, enc_keys, enc_values, enc_mixed, enc_mixed_grad, enc_log
    )
    enc_input_grad = to_half(
        enc_one_grad
        + mm_t(enc_dq, enc_mats[0])
        + mm_t(enc_dk, enc_mats[1])
        + mm_t(enc_dv, enc_mats[2])
    )
    vec_grads = jnp.stack(
        [
            column_sum(enc_dq),
            column_sum(enc_dv),
            column_sum(enc_one_grad),
            enc_gain_one,
            enc_shift_one,
            column_sum(enc_two_grad),
            enc_gain_two,
            enc_shift_two,
            column_sum(self_dq),
            column_sum(self_dv),
            column_sum(sum_one_grad),
            gain_one,
            shift_one,
            column_sum(cross_dq),
            column_sum(cross_dv),
            column_sum(sum_two_grad),
            gain_two,
            shift_two,
            column_sum(sum_three_grad),
            gain_three,
            shift_three,
        ]
    )
    small_grad = pad_rows(
        jnp.concatenate(
            [
                pad_rows(query_grad, vec_at),
                pad_rows(vec_grads, head_at - vec_at),
                head_grad_t,
            ]
        ),
        n_small,
    ).T
    bias_grad = jnp.concatenate([column_sum(enc_inner_half), column_sum(dec_inner_half)])
    bias_grad = pad_columns(bias_grad.reshape(devices, bias_part), shard * 128).reshape(width, 128)
    enc_sums = scatter(
        jnp.concatenate(
            [
                to_half(g)
                for g in (
                    t_mm(enc_in, enc_dq),
                    t_mm(enc_in, enc_dk),
                    t_mm(enc_x, enc_dv),
                    enc_out_wgrad,
                    enc_expand_grad,
                    enc_reduce_grad_t,
                    small_grad,
                    bias_grad,
                )
            ],
            axis=1,
        )
    )

    def to_parts(values, part):
        return lax.all_to_all(values.reshape(per_rank, ranks * part, width), "seq", 1, 0, tiled=True)

    outputs = [to_parts(enc_input_grad, enc_part), to_parts(dec_input_grad, dec_part)]

    at = 4 * width
    small_sum = enc_sums[:, at + 2 * width_ff : at + 2 * width_ff + n_small]
    bias_sum = enc_sums[:, at + 2 * width_ff + n_small :]
    gradients = (
        jnp.stack(
            [enc_sums[:, i * width : (i + 1) * width] for i in range(4)]
            + [dec_sums[:, i * width : (i + 1) * width] for i in range(8)]
        ),
        jnp.stack([enc_sums[:, at : at + width_ff], dec_sums[:, 2 * at : 2 * at + width_ff]]),
        jnp.swapaxes(
            jnp.stack(
                [enc_sums[:, at + width_ff : at + 2 * width_ff], dec_sums[:, 2 * at + width_ff :]]
            ),
            1,
            2,
        ),
        small_sum[:, head_at : head_at + joints],
        small_sum[:, :n_query].T,
        small_sum[:, vec_at : vec_at + n_vec].T,
        bias_sum.reshape(-1)[:bias_part],
    )
    weights = (
        attention_mats,
        expand_mats,
        reduce_mats,
        action_head,
        query_pos,
        vectors,
        expand_bias,
    )
    firsts, seconds = moments[:7], moments[7:]
    rates = (rate_matrix,) * 4 + (rate_vector,) * 3
    for weight, gradient, moment_one, moment_two, step_rate in zip(
        weights, gradients, firsts, seconds, rates
    ):
        outputs.extend(adamw(weight, gradient, moment_one, moment_two, step_rate))
    return tuple(outputs)


def solution(mesh):
    rows = P("dp", "seq", None)
    weight_specs = (
        P(None, ALL, None),
        P(None, ALL, None),
        P(None, None, ALL),
        P(ALL, None),
        P(None, ALL),
        P(None, ALL),
        P(ALL),
    )
    in_specs = (rows, rows, rows, P("dp")) + weight_specs * 3
    out_specs = (rows, rows) + tuple(spec for spec in weight_specs for unused in range(4))
    return jax.shard_map(
        per_device, mesh=mesh, in_specs=in_specs, out_specs=out_specs, check_vma=False
    )
```

time: 2530 us -> 857 us (0.34)
  waiting for transfers between devices: 1460 us -> 431 us
  blocking collectives: 548 us -> 10.6 us
  matrix products: 297 us -> 203 us
  local copies, waits for them, and re-layouts: 152 us -> 76.1 us
  Pallas kernels: 0 us -> 53.4 us
    reduce_scatter x8 -> x2, waiting for transfers between devices: 1020 us -> 284 us  [scatter(): lax.psum_scatter(columns, ALL, scatter_dimension=0, tiled=True).astype(F32)]
    all_gather x16 -> x0, blocking collectives: 467 us -> none  [the longest x1 71.5 us: per_device(): lax.all_gather(dec_local[3], ('dp', 'seq'), axis=0, tiled=True)]
    unnamed x24 -> x4, waiting for transfers between devices: 260 us -> 0.73 us
    all_gather x12 -> x2, waiting for transfers between devices: 174 us -> 64.6 us  [gather(): return lax.all_gather(columns, ALL, axis=0, tiled=True)]
    dot_general x99 -> x61, matrix products: 297 us -> 196 us  [the longest x17 55.3 us: t_mm(): lax.dot_general(a, b, (((0,), (0,)), ((), ())), preferred_element_type=F32)]
    all_to_all x0 -> x4, waiting for transfers between devices: none -> 81.4 us  [the longest x2 45.6 us: to_parts(): lax.all_to_all(values.reshape(per_rank, ranks * part, width), 'seq', 1, 0...]
    unnamed x2 -> x0, blocking collectives: 81.1 us -> none
    dynamic_slice x53 -> x1, local copies, waits for them, and re-layouts: 57.9 us -> 0.59 us  [per_device(): length = lengths[seq_index]]
  transfers between devices with their start and end apart: 22 -> 8, of which waited for: 14 -> 7; matrix products, arithmetic and copies ran while one was open for 18% -> 10% of each run, Pallas kernels for 0% -> 3%
where the time goes in v1:
time: 857 us; the launch traced here: 846 us
  waiting for transfers between devices  431 us (50%)
  matrix products  203 us (24%)
  local copies, waits for them, and re-layouts  76.1 us (9%)
  Pallas kernels  53.4 us (6%)
  other arithmetic  37.5 us (4%)
  starting transfers between devices  19.3 us (2%)
  between operations  15.5 us (2%)
  blocking collectives  10.6 us (1%)
    reduce_scatter x2, waiting for transfers between devices, scatter(): lax.psum_scatter(columns, ALL, scatter_dimension=0, tiled=True).astype(F32)  284 us
    all_gather x2, waiting for transfers between devices, gather(): return lax.all_gather(columns, ALL, axis=0, tiled=True)  64.6 us
    dot_general x17, matrix products, t_mm(): lax.dot_general(a, b, (((0,), (0,)), ((), ())), preferred_element_type=F32)  55.3 us
    dot_general x17, matrix products, mm(): lax.dot_general(a, b, (((1,), (0,)), ((), ())), preferred_element_type=F32)  52.3 us
    dot_general x17, matrix products, mm_t(): lax.dot_general(a, b, (((1,), (1,)), ((), ())), preferred_element_type=F32)  46.4 us
    all_to_all x2, waiting for transfers between devices, to_parts(): lax.all_to_all(values.reshape(per_rank, ranks * part, width), 'seq', 1, 0...  45.6 us
    all_to_all x2, waiting for transfers between devices, to_item(): return lax.all_to_all(values, 'seq', 0, 1, tiled=True)  35.8 us
    pallas_call x1, Pallas kernels, attend(): pl.pallas_call(functools.partial(attend_kernel, chunk=256), grid=(pairs,)...  26.8 us
  transfers between devices with their start and end apart: 8, of which 7 were waited for; matrix products, arithmetic and copies ran while one was open for 10% of the time, Pallas kernels for 3%

profile of v1, /device:TPU:0, one launch (start us, length us, event | category | flops | bytes accessed | tf_op | source)
XLA Modules:
  0.0 845.7 jit_solution(16463607064749657270)
XLA Ops:
  15.7 6.3 all-to-all-start.2
  22.0 5.6 all-to-all-done.2
  27.6 10.6 %all_to_all.51 = bf16[4,25,512]{2,1,0:T(8,128)(2,1)S(1)} all-to-all(bf16[4,25,512]{2,1,0:T(8,128)(2,1)S(1)} %copy.189), channel_id=1, replica_groups=mesh['dp'=8,'seq'=4] {'seq'}, dimensions={0} | all-to-all | bytes 204800 | tf_op jit(solution)/shard_map/all_to_all | solution.py:293
  38.1 4.3 all-to-all-start
  45.6 30.2 %all-to-all-done = bf16[4,256,512]{2,1,0:T(8,128)(2,1)} async-done(((bf16[4,256,512]{2,1,0:T(8,128)(2,1)}), bf16[4,256,512]{2,1,0:T(8,128)(2,1)}, u32[]{:S(2)}, u32[]{:S(2)}) %all-to-all-start) | async-done | bytes 1048608 | tf_op jit(solution)/shard_map/all_to_all | solution.py:293
  77.3 33.9 %all-gather.3.cloned.1.call-done = bf16[512,8832]{1,0:T(8,128)(2,1)} async-done(((bf16[16,8832]{1,0:T(8,128)(2,1)}), bf16[512,8832]{1,0:T(8,128)(2,1)}) %all-gather.3.cloned.1.call-update) | async-done | bytes 9043984 | tf_op jit(solution)/shard_map/all_gather | solution.py:233
  125.3 26.8 %shard_map.481 = (bf16[1024,512]{1,0:T(8,128)(2,1)S(1)}, f32[4,2,1024]{2,1,0:T(2,128)S(1)}) custom-call(bf16[1024,512]{1,0:T(8,128)(2,1)S(1)} %add_convert_fusion.4.q_ref, bf16[1024,512]{1,0:T(8,128)(2,1)S(1)} %convolution_convert_fusion.7.k_ref, bf16[1024,512]{1,0:T(8,128)(2,1)S(1)} %fusion.56.v_ref), custom_call_target="tpu_custom_call" | custom-call | flops 8589934592 | bytes 4194304 | tf_op jit(solution)/shard_map/pallas_call | solution.py:109
  153.3 6.9 fusion.29
  160.2 9.2 %fusion.232 = (f32[1024]{0:T(1024)S(1)}, f32[1024,512]{0,1:T(8,128)S(1)}) fusion(f32[512]{0:T(512)S(1)} %bitcast.399, bf16[512,8832]{1,0:T(8,128)(2,1)S(1)} %bitcast.324, f32[1024,3200]{1,0:T(8,128)} %fusion.29, f32[3200]{0:T(1024)S(1)} %slice.296, f32[512]{0:T(512)S(1)} %bitcast.392, f32[512]{0:T(512)S(1)} %bitcast.380, f32[1024]{0:T(1024)S(1)} %add_rsqrt_fusion.1, ...), kind=kOutput, calls=%fused_computation.411 | convolution fusion | flops 3391880192 | bytes 20613120 | tf_op jit(solution)/shard_map/dot_general | solution.py:38
  170.8 30.6 %all-gather.5.cloned.1.call-done = bf16[512,10496]{1,0:T(8,128)(2,1)} async-done(((bf16[16,10496]{1,0:T(8,128)(2,1)}), bf16[512,10496]{1,0:T(8,128)(2,1)}) %all-gather.5.cloned.1.call-update) | async-done | bytes 10747920 | tf_op jit(solution)/shard_map/all_gather | solution.py:233
  219.1 3.6 convolution_convert_fusion.6
  222.6 4.7 fusion.233
  248.7 4.3 fusion.242
  255.4 11.1 %fusion.239 = (bf16[8,64]{1,0:T(8,128)(2,1)}, bf16[8,64,100]{2,1,0:T(8,128)(2,1)}) fusion(bf16[1024,8,64]{0,2,1:T(8,128)(2,1)} %bitcast.315, f32[8,100,1024]{2,1,0:T(8,128)} %fusion.245, f32[8,100,1024]{2,1,0:T(8,128)} %get-tuple-element.267, f32[8,100]{1,0:T(8,128)S(1)} %copy-done.91), kind=kOutput, calls=%fused_computation.416 | convolution fusion | flops 110695712 | bytes 7708800 | tf_op jit(solution)/shard_map/hqk,khd->qhd/dot_general | solution.py:199
  266.5 10.6 %fusion.53 = bf16[8,64,1024]{2,1,0:T(8,128)(2,1)} fusion(bf16[100,8,64]{0,2,1:T(8,128)(2,1)} %bitcast.345, f32[8,100,1024]{2,1,0:T(8,128)} %fusion.245, f32[8,100,1024]{2,1,0:T(8,128)} %get-tuple-element.267, f32[8,100]{1,0:T(8,128)S(1)} %copy-done.91), kind=kOutput, calls=%fused_computation.79 | convolution fusion | flops 111118112 | bytes 7707776 | tf_op jit(solution)/shard_map/hqk,qhd->khd/dot_general | solution.py:200
  292.1 3.0 fusion.236
  297.3 3.0 multiply_reduce_fusion.2
  301.7 17.2 %fusion.244 = (bf16[3200]{0:T(1024)(128)(2,1)}, bf16[1024,3200]{1,0:T(8,128)(2,1)S(1)}) fusion(f32[1024,3200]{1,0:T(8,128)} %fusion.29, f32[3200]{0:T(1024)S(1)} %copy-done.65, bf16[512,8832]{1,0:T(8,128)(2,1)} %all-gather.3.cloned.1.call-done, f32[1024,512]{0,1:T(8,128)S(1)} %get-tuple-element.215), kind=kOutput, calls=%fused_computation.419 | convolution fusion | flops 3428054016 | bytes 25053952 | tf_op jit(solution)/shard_map/dot_general | solution.py:34
  318.9 9.2 %multiply_reduce_fusion.3 = (bf16[512]{0:T(512)(128)(2,1)}, f32[1024]{0:T(1024)S(1)}, f32[1024]{0:T(1024)S(1)}, bf16[512]{0:T(512)(128)(2,1)}, f32[1024,512]{0,1:T(8,128)S(1)}) fusion(f32[1024,512]{0,1:T(8,128)S(1)} %copy-done.13, f32[1024]{0:T(1024)S(1)} %copy-done.63, f32[1024]{0:T(1024)S(1)} %broadcast_multiply_fusion.5, f32[512]{0:T(512)S(1)} %bitcast.381, ...), kind=kOutput, calls=%fused_computation.48 | convolution fusion | flops 3360683008 | bytes 16142336 | tf_op jit(solution)/shard_map/dot_general | solution.py:38
  333.8 26.6 %shard_map.482 = (bf16[1024,512]{1,0:T(8,128)(2,1)S(1)}, bf16[1024,512]{1,0:T(8,128)(2,1)S(1)}, bf16[1024,512]{1,0:T(8,128)(2,1)S(1)}) custom-call(bf16[1024,512]{1,0:T(8,128)(2,1)S(1)} %copy-done.4, bf16[1024,512]{1,0:T(8,128)(2,1)S(1)} %copy-done.2, bf16[1024,512]{1,0:T(8,128)(2,1)} %copy-done.5, bf16[1024,512]{1,0:T(8,128)(2,1)} %copy-done, ...), custom_call_target="tpu_custom_call" | custom-call | flops 21474836480 | bytes 8388608 | tf_op jit(solution)/shard_map/pallas_call | solution.py:167
  364.8 3.5 convolution_convert_fusion.19
  405.6 3.4 convolution_convert_fusion.18
  420.0 8.9 %fusion.14 = bf16[512,8832]{1,0:T(8,128)(2,1)} fusion(bf16[512,8832]{1,0:T(8,128)(2,1)} %constant_dynamic-update-slice_fusion.16, bf16[1024,3200]{1,0:T(8,128)(2,1)} %copy-done.105, f32[1024,512]{0,1:T(8,128)S(1)} %copy-done.14, f32[512]{0:T(512)S(1)} %bitcast.393, f32[512]{0:T(512)S(1)} %bitcast.383, f32[1024]{0:T(1024)S(1)} %copy-done.63, ...), kind=kOutput, calls=%fused_computation.21 | convolution fusion | flops 3359703040 | bytes 11939840 | tf_op jit(solution)/shard_map/dot_general | solution.py:42
  428.9 12.1 %fusion.13 = bf16[512,8832]{1,0:T(8,128)(2,1)} fusion(bf16[512,8832]{1,0:T(8,128)(2,1)} %fusion.14, f32[1024,512]{0,1:T(8,128)S(1)} %copy-done.25, f32[1024,3200]{1,0:T(8,128)} %fusion.29, f32[3200]{0:T(1024)S(1)} %copy-done.66), kind=kOutput, calls=%fused_computation.19 | convolution fusion | flops 3390373888 | bytes 18493952 | tf_op jit(solution)/shard_map/dot_general | solution.py:42
  453.4 3.5 fusion.69
  459.9 2.9 fusion.11
  470.6 3.5 all-to-all-start.4
  481.5 7.0 reduce.24
  490.5 5.1 all-to-all-start.3
  497.1 45.6 %all-to-all-done.3 = bf16[4,2,65536]{2,1,0:T(2,128)(2,1)S(1)} async-done(((bf16[4,2,65536]{2,1,0:T(2,128)(2,1)}), bf16[4,2,65536]{2,1,0:T(2,128)(2,1)S(1)}, u32[]{:S(2)}, u32[]{:S(2)}) %all-to-all-start.3) | async-done | bytes 1048608 | tf_op jit(solution)/shard_map/all_to_all | solution.py:490
  545.0 51.9 %reduce-scatter.3.cloned.1.call-done = bf16[16,8832]{1,0:T(8,128)(2,1)} async-done(((bf16[512,8832]{1,0:T(8,128)(2,1)}), bf16[16,8832]{1,0:T(8,128)(2,1)}) %reduce-scatter.3.cloned.1.call-update) | async-done | bytes 282640 | tf_op jit(solution)/shard_map/reduce_scatter | solution.py:237
  600.6 232.2 %reduce-scatter.5.cloned.1.call-done = bf16[16,10496]{1,0:T(8,128)(2,1)} async-done(((bf16[512,10496]{1,0:T(8,128)(2,1)}), bf16[16,10496]{1,0:T(8,128)(2,1)}) %reduce-scatter.5.cloned.1.call-update) | async-done | bytes 335888 | tf_op jit(solution)/shard_map/reduce_scatter | solution.py:237
  (439 shorter events, 193.1 us)
Async XLA Ops:
  7.2 104.0 %all-gather.3.cloned.1.call-start = ((), (), s32[]{:S(2)}) async-start(), calls=%async_computation.7 | async-start | bytes 9326592 | tf_op jit(solution)/shard_map/all_gather | solution.py:233
  14.2 187.2 %all-gather.5.cloned.1.call-start = ((), (), s32[]{:S(2)}) async-start(), calls=%async_computation.8 | async-start | bytes 11083776 | tf_op jit(solution)/shard_map/all_gather | solution.py:233
  15.7 11.9 %all-to-all-start.2 = ((f32[4,1,350]{2,1,0:T(1,128)}), f32[4,1,350]{2,1,0:T(1,128)S(1)}, u32[]{:S(2)}, u32[]{:S(2)}) async-start(f32[4,1,350]{2,1,0:T(1,128)} %reshape.286), calls=%async_computation.2 | async-start | bytes 12288 | tf_op jit(solution)/shard_map/all_to_all | solution.py:293
  38.1 37.7 %all-to-all-start = ((bf16[4,256,512]{2,1,0:T(8,128)(2,1)}), bf16[4,256,512]{2,1,0:T(8,128)(2,1)}, u32[]{:S(2)}, u32[]{:S(2)}) async-start(bf16[4,256,512]{2,1,0:T(8,128)(2,1)} %param.26), calls=%async_computation | async-start | bytes 2097152 | tf_op jit(solution)/shard_map/all_to_all | solution.py:293
  42.4 554.5 %reduce-scatter.3.cloned.1.call-start = ((), (), s32[]{:S(2)}) async-start(), calls=%async_computation.9 | async-start | bytes 9326592 | tf_op jit(solution)/shard_map/reduce_scatter | solution.py:237
  77.3 74.8 %copy-start.11 = (bf16[1024,512]{0,1:T(8,128)(2,1)}, bf16[1024,512]{0,1:T(8,128)(2,1)S(1)}, u32[]{:S(2)}) copy-start(bf16[1024,512]{0,1:T(8,128)(2,1)S(1)} %copy.244) | copy-start | bytes 3145732
  77.3 43.4 %copy-start.10 = (f32[1024,512]{0,1:T(8,128)S(1)}, f32[1024,512]{0,1:T(8,128)}, u32[]{:S(2)}) copy-start(f32[1024,512]{0,1:T(8,128)} %constant.66.clone) | copy-start | bytes 6291460
  113.8 46.3 %copy-start.64 = (f32[3200]{0:T(1024)}, f32[3200]{0:T(1024)S(1)}, u32[]{:S(2)}) copy-start(f32[3200]{0:T(1024)S(1)} %slice.296) | copy-start | bytes 38404
  118.7 41.5 %copy-start.70 = (f32[1,512]{1,0:T(1,128)}, f32[1,512]{1,0:T(1,128)S(1)}, u32[]{:S(2)}) copy-start(f32[1,512]{1,0:T(1,128)S(1)} %get-tuple-element.252) | copy-start | bytes 6148
  118.7 41.5 %copy-start.93 = (f32[1,512]{1,0:T(1,128)}, f32[1,512]{1,0:T(1,128)S(1)}, u32[]{:S(2)}) copy-start(f32[1,512]{1,0:T(1,128)S(1)} %get-tuple-element.251) | copy-start | bytes 6148
  152.1 177.3 %copy-start = (bf16[1024,512]{1,0:T(8,128)(2,1)}, bf16[1024,512]{1,0:T(8,128)(2,1)S(1)}, u32[]{:S(2)}) copy-start(bf16[1024,512]{1,0:T(8,128)(2,1)S(1)} %get-tuple-element.35.o_ref) | copy-start | bytes 3145732
  169.4 130.9 %copy-start.8 = (f32[1024,512]{0,1:T(8,128)}, f32[1024,512]{0,1:T(8,128)S(1)}, u32[]{:S(2)}) copy-start(f32[1024,512]{0,1:T(8,128)S(1)} %get-tuple-element.265) | copy-start | bytes 6291460
  442.5 390.3 %reduce-scatter.5.cloned.1.call-start = ((), (), s32[]{:S(2)}) async-start(), calls=%async_computation.10 | async-start | bytes 11083776 | tf_op jit(solution)/shard_map/reduce_scatter | solution.py:237
  470.6 20.0 %all-to-all-start.4 = ((bf16[4,2,6400]{2,1,0:T(2,128)(2,1)}), bf16[4,2,6400]{2,1,0:T(2,128)(2,1)S(1)}, u32[]{:S(2)}, u32[]{:S(2)}) async-start(bf16[4,2,6400]{2,1,0:T(2,128)(2,1)} %reshape.290), calls=%async_computation.4 | async-start | bytes 204800 | tf_op jit(solution)/shard_map/all_to_all | solution.py:490
  490.5 52.2 %all-to-all-start.3 = ((bf16[4,2,65536]{2,1,0:T(2,128)(2,1)}), bf16[4,2,65536]{2,1,0:T(2,128)(2,1)S(1)}, u32[]{:S(2)}, u32[]{:S(2)}) async-start(bf16[4,2,65536]{2,1,0:T(2,128)(2,1)} %reshape.288), calls=%async_computation.3 | async-start | bytes 2097152 | tf_op jit(solution)/shard_map/all_to_all | solution.py:490
  497.0 100.8 %copy-start.96 = (f32[200]{0:T(256)S(1)}, f32[200]{0:T(256)}, u32[]{:S(2)}) copy-start(f32[200]{0:T(256)} %param.36) | copy-start | bytes 2404
  497.0 100.8 %copy-start.97 = (f32[200]{0:T(256)S(1)}, f32[200]{0:T(256)}, u32[]{:S(2)}) copy-start(f32[200]{0:T(256)} %param.50) | copy-start | bytes 2404
  497.0 100.8 %copy-start.98 = (f32[200]{0:T(256)S(1)}, f32[200]{0:T(256)}, u32[]{:S(2)}) copy-start(f32[200]{0:T(256)} %param.43) | copy-start | bytes 2404
  497.0 101.4 %copy-start.57 = (f32[16,14]{1,0:T(8,128)S(1)}, f32[16,14]{1,0:T(8,128)}, u32[]{:S(2)}) copy-start(f32[16,14]{1,0:T(8,128)} %param.33) | copy-start | bytes 2692
  497.0 101.4 %copy-start.77 = (f32[16,14]{1,0:T(8,128)S(1)}, f32[16,14]{1,0:T(8,128)}, u32[]{:S(2)}) copy-start(f32[16,14]{1,0:T(8,128)} %param.47) | copy-start | bytes 2692
  497.0 101.4 %copy-start.78 = (f32[16,14]{1,0:T(8,128)S(1)}, f32[16,14]{1,0:T(8,128)}, u32[]{:S(2)}) copy-start(f32[16,14]{1,0:T(8,128)} %param.40) | copy-start | bytes 2692
  497.1 102.1 %copy-start.58 = (f32[21,16]{0,1:T(8,128)S(1)}, f32[21,16]{0,1:T(8,128)}, u32[]{:S(2)}) copy-start(f32[21,16]{0,1:T(8,128)} %param.35) | copy-start | bytes 4036
  497.1 102.1 %copy-start.79 = (f32[21,16]{0,1:T(8,128)S(1)}, f32[21,16]{0,1:T(8,128)}, u32[]{:S(2)}) copy-start(f32[21,16]{0,1:T(8,128)} %param.49) | copy-start | bytes 4036
  497.1 102.1 %copy-start.80 = (f32[21,16]{0,1:T(8,128)S(1)}, f32[21,16]{0,1:T(8,128)}, u32[]{:S(2)}) copy-start(f32[21,16]{0,1:T(8,128)} %param.42) | copy-start | bytes 4036
  497.1 102.8 %copy-start.59 = (f32[100,16]{0,1:T(8,128)S(1)}, f32[100,16]{0,1:T(8,128)}, u32[]{:S(2)}) copy-start(f32[100,16]{0,1:T(8,128)} %param.34) | copy-start | bytes 19204
  497.1 102.8 %copy-start.81 = (f32[100,16]{0,1:T(8,128)S(1)}, f32[100,16]{0,1:T(8,128)}, u32[]{:S(2)}) copy-start(f32[100,16]{0,1:T(8,128)} %param.48) | copy-start | bytes 19204
  497.1 102.7 %copy-start.82 = (f32[100,16]{0,1:T(8,128)S(1)}, f32[100,16]{0,1:T(8,128)}, u32[]{:S(2)}) copy-start(f32[100,16]{0,1:T(8,128)} %param.41) | copy-start | bytes 19204
  543.7 290.3 %copy-start.29 = (f32[12,16,512]{2,1,0:T(8,128)S(1)}, f32[12,16,512]{2,1,0:T(8,128)}, u32[]{:S(2)}) copy-start(f32[12,16,512]{2,1,0:T(8,128)} %param.30) | copy-start | bytes 1179652
  543.7 290.3 %copy-start.53 = (f32[12,16,512]{2,1,0:T(8,128)S(1)}, f32[12,16,512]{2,1,0:T(8,128)}, u32[]{:S(2)}) copy-start(f32[12,16,512]{2,1,0:T(8,128)} %param.44) | copy-start | bytes 1179652
  598.5 237.9 %copy-start.27 = (f32[2,3200,16]{1,2,0:T(8,128)S(1)}, f32[2,3200,16]{1,2,0:T(8,128)}, u32[]{:S(2)}) copy-start(f32[2,3200,16]{1,2,0:T(8,128)} %param.32) | copy-start | bytes 1228804
  598.5 237.9 %copy-start.49 = (f32[2,3200,16]{1,2,0:T(8,128)S(1)}, f32[2,3200,16]{1,2,0:T(8,128)}, u32[]{:S(2)}) copy-start(f32[2,3200,16]{1,2,0:T(8,128)} %param.46) | copy-start | bytes 1228804
  598.5 237.9 %copy-start.50 = (f32[2,3200,16]{1,2,0:T(8,128)S(1)}, f32[2,3200,16]{1,2,0:T(8,128)}, u32[]{:S(2)}) copy-start(f32[2,3200,16]{1,2,0:T(8,128)} %param.39) | copy-start | bytes 1228804
  (88 other events, 730.7 us)
Sparse Core Ops, SparseCore 0:
  14.3 96.9 all-gather.2
  114.7 86.6 all-gather.4
  442.6 154.2 reduce-scatter.2
  599.1 233.6 reduce-scatter.4

commit v2 on v1

v2 whole, which is shorter than its diff:
```python
import functools
import math

import jax
import jax.numpy as jnp
import numpy as np
from jax import lax
from jax.experimental import pallas as pl
from jax.experimental.pallas import tpu as pltpu
from jax.sharding import PartitionSpec as P

HEADS = 8
HDIM = 64
PAIR = 2 * HDIM
STEP = 10
ALL = ("dp", "seq")

beta_first = 0.9
beta_second = 0.999
epsilon = 1e-08
decay_rate = 0.1
rate_matrix = 0.08
rate_vector = 0.2

BF = jnp.bfloat16
F32 = jnp.float32
MB = 1 << 20
SCALE = HDIM ** (-0.5)


def to_half(values):
    return values.astype(BF)


def mm(a, b):
    return lax.dot_general(a, b, (((1,), (0,)), ((), ())), preferred_element_type=F32)


def mm_t(a, b):
    return lax.dot_general(a, b, (((1,), (1,)), ((), ())), preferred_element_type=F32)


def column_sum(values):
    return jnp.sum(values.astype(F32), axis=0, keepdims=True)


def norm_parts(values):
    center = values - jnp.mean(values, axis=-1, keepdims=True)
    scale = lax.rsqrt(jnp.mean(center * center, axis=-1, keepdims=True) + 1e-05)
    return center * scale, scale


def layer_norm(values, gain, shift):
    return norm_parts(values)[0] * gain + shift


def norm_back(values, gain, gradient):
    unit, scale = norm_parts(values)
    inner = gradient * gain
    mean_inner = jnp.mean(inner, axis=-1, keepdims=True)
    mean_cross = jnp.mean(inner * unit, axis=-1, keepdims=True)
    back = scale * (inner - mean_inner - unit * mean_cross)
    return back, column_sum(gradient * unit), column_sum(gradient)


GELU_A = math.sqrt(2.0 / math.pi)
GELU_B = 0.044715


def gelu_parts(u):
    square = u * u
    bend = jnp.tanh(u * (GELU_A + GELU_A * GELU_B * square))
    half = 0.5 + 0.5 * bend
    slope = half + (0.5 * u) * (1.0 - bend * bend) * (GELU_A + 3.0 * GELU_A * GELU_B * square)
    return u * half, slope


def gelu(u):
    return u * (0.5 + 0.5 * jnp.tanh(u * (GELU_A + GELU_A * GELU_B * (u * u))))


def sine_table(count, width):
    halves = np.arange(width // 2, dtype=np.float64)
    frequency = np.exp(halves * (-2.0 * math.log(10000.0) / width))
    angles = np.arange(count)[:, None] * frequency[None, :]
    table = np.stack([np.sin(angles), np.cos(angles)], axis=-1).reshape(count, width)
    return table.astype(np.float32)


def own_lanes(values, h):
    lane = lax.broadcasted_iota(jnp.int32, values.shape, 1)
    return jnp.where((lane < HDIM) == (h == 0), values, jnp.zeros_like(values))


def join_rows(first, second):
    row = lax.broadcasted_iota(jnp.int32, first.shape, 0)
    return jnp.where(row < HDIM, first, second)


def attend_kernel(
    x_ref, pos_ref, wq_ref, wk_ref, wv_ref, vec_ref, q_ref, k_ref, v_ref, o_ref, log_ref, in_ref, vt_ref, *, chunk
):
    @pl.when(pl.program_id(0) == 0)
    def _():
        in_ref[...] = to_half(x_ref[...].astype(F32) + pos_ref[...])

    q_ref[...] = to_half(mm(in_ref[...], wq_ref[...]) + vec_ref[0:1, :])
    k_ref[...] = to_half(mm(in_ref[...], wk_ref[...]))
    values = to_half(mm(x_ref[...], wv_ref[...]) + vec_ref[1:2, :])
    v_ref[...] = values
    vt_ref[...] = values.T

    def step(i, carry):
        at = pl.ds(i * chunk, chunk)
        query = q_ref[at, :] * BF(SCALE)
        mixed = []
        for h in range(2):
            scores = mm_t(k_ref[...], own_lanes(query, h))
            peak = jnp.max(scores, axis=0, keepdims=True)
            weights = jnp.exp(scores - peak)
            total = jnp.sum(weights, axis=0, keepdims=True)
            mixed.append(mm(vt_ref[...], to_half(weights)) / total)
            log_ref[0, pl.ds(h, 1), at] = peak + jnp.log(total)
        o_ref[at, :] = to_half(join_rows(*mixed).T)
        return carry

    lax.fori_loop(0, q_ref.shape[0] // chunk, step, 0)


def attend(x, positions, weights, vec):
    rows, width = x.shape
    pairs = width // PAIR
    whole = pl.BlockSpec((rows, width), lambda i: (0, 0))
    own = pl.BlockSpec((rows, PAIR), lambda i: (0, i))
    mats = [pl.BlockSpec((width, PAIR), lambda i, j=j: (0, i + j * pairs)) for j in range(3)]
    half = jax.ShapeDtypeStruct((rows, width), BF)
    return pl.pallas_call(
        functools.partial(attend_kernel, chunk=256),
        grid=(pairs,),
        in_specs=[whole, whole] + mats + [pl.BlockSpec((vec.shape[0], PAIR), lambda i: (0, i))],
        out_specs=[own] * 4 + [pl.BlockSpec((1, 2, rows), lambda i: (i, 0, 0))],
        out_shape=[half] * 4 + [jax.ShapeDtypeStruct((pairs, 2, rows), F32)],
        scratch_shapes=[pltpu.VMEM((rows, width), BF), pltpu.VMEM((PAIR, rows), BF)],
        compiler_params=pltpu.CompilerParams(vmem_limit_bytes=56 * MB),
        cost_estimate=pl.CostEstimate(
            flops=16 * rows * rows * width, bytes_accessed=12 * rows * width, transcendentals=8 * rows * rows
        ),
        name="attend",
    )(x, positions, weights, weights, weights, vec)


def forward_kernel(
    mixed_ref, x_ref, out_ref, vec_ref, e_ref, r_ref, bias_ref,
    sum_one_ref, hidden_ref, u_ref, sum_two_ref, memory_ref, *, tile
):
    step = pl.program_id(0)
    count = x_ref.shape[0] // tile

    def rows_of(i):
        return pl.ds(pl.multiple_of(i * tile, tile), tile)

    @pl.when(step == 0)
    def _():
        def body(i, carry):
            at = rows_of(i)
            total = x_ref[at, :].astype(F32) + mm(mixed_ref[at, :], out_ref[...]) + vec_ref[2:3, :]
            sum_one_ref[at, :] = total
            hidden = layer_norm(total, vec_ref[3:4, :], vec_ref[4:5, :])
            hidden_ref[at, :] = to_half(hidden)
            sum_two_ref[at, :] = hidden + vec_ref[5:6, :]
            return carry

        lax.fori_loop(0, count, body, 0)

    def body(i, carry):
        at = rows_of(i)
        u = mm(hidden_ref[at, :], e_ref[...]) + bias_ref[...]
        u_ref[at, :] = u
        sum_two_ref[at, :] += mm_t(to_half(gelu(u)), r_ref[...])
        return carry

    lax.fori_loop(0, count, body, 0)

    @pl.when(step == pl.num_programs(0) - 1)
    def _():
        def body(i, carry):
            at = rows_of(i)
            memory_ref[at, :] = layer_norm(sum_two_ref[at, :], vec_ref[6:7, :], vec_ref[7:8, :])
            return carry

        lax.fori_loop(0, count, body, 0)


def feed_forward(mixed, x, enc_mats, vec, enc_ffn, bias):
    rows, width = x.shape
    width_ff = bias.shape[1]
    block = 640 if width_ff % 640 == 0 else width_ff
    steps = width_ff // block
    whole = pl.BlockSpec((rows, width), lambda i: (0, 0))
    float_rows = jax.ShapeDtypeStruct((rows, width), F32)
    return pl.pallas_call(
        functools.partial(forward_kernel, tile=256),
        grid=(steps,),
        in_specs=[
            whole,
            whole,
            pl.BlockSpec((width, width), lambda i: (0, 3)),
            pl.BlockSpec(vec.shape, lambda i: (0, 0)),
            pl.BlockSpec((width, block), lambda i: (0, i)),
            pl.BlockSpec((width, block), lambda i: (0, i + steps)),
            pl.BlockSpec((1, block), lambda i: (0, i)),
        ],
        out_specs=[whole, whole, pl.BlockSpec((rows, block), lambda i: (0, i)), whole, whole],
        out_shape=[
            float_rows,
            jax.ShapeDtypeStruct((rows, width), BF),
            jax.ShapeDtypeStruct((rows, width_ff), F32),
            float_rows,
            float_rows,
        ],
        compiler_params=pltpu.CompilerParams(vmem_limit_bytes=56 * MB),
        cost_estimate=pl.CostEstimate(
            flops=4 * rows * width * width_ff, bytes_accessed=4 * rows * width_ff, transcendentals=rows * width_ff
        ),
        name="feed_forward",
    )(mixed, x, enc_mats, vec, enc_ffn, enc_ffn, bias)


def turned(turn, values):
    return to_half(mm_t(turn, values))


def lefts_kernel(x_ref, pos_ref, mixed_ref, hidden_ref, turn_ref, in_t_ref, x_t_ref, mixed_t_ref, hidden_t_ref):
    in_t_ref[...] = turned(turn_ref[...], to_half(x_ref[...].astype(F32) + pos_ref[...]))
    x_t_ref[...] = turned(turn_ref[...], x_ref[...])
    mixed_t_ref[...] = turned(turn_ref[...], mixed_ref[...])
    hidden_t_ref[...] = turned(turn_ref[...], hidden_ref[...])


def lefts(x, positions, mixed, hidden, turn):
    rows, width = x.shape
    return pl.pallas_call(
        lefts_kernel,
        out_shape=[jax.ShapeDtypeStruct((width, rows), BF)] * 4,
        compiler_params=pltpu.CompilerParams(vmem_limit_bytes=40 * MB),
        cost_estimate=pl.CostEstimate(flops=8 * rows * width * width, bytes_accessed=20 * rows * width, transcendentals=0),
        name="lefts",
    )(x, positions, mixed, hidden, turn)


def norm_kernel(grad_ref, sum_two_ref, vec_ref, turn_ref, two_ref, half_t_ref, vec_grad_ref, half_ref, *, tile):
    vec_grad_ref[...] = jnp.zeros_like(vec_grad_ref)

    def body(i, carry):
        at = pl.ds(pl.multiple_of(i * tile, tile), tile)
        back, gain, shift = norm_back(sum_two_ref[at, :], vec_ref[6:7, :], grad_ref[at, :])
        two_ref[at, :] = back
        half_ref[at, :] = to_half(back)
        vec_grad_ref[0:1, :] += column_sum(back)
        vec_grad_ref[1:2, :] += gain
        vec_grad_ref[2:3, :] += shift
        return carry

    lax.fori_loop(0, grad_ref.shape[0] // tile, body, 0)
    half_t_ref[...] = turned(turn_ref[...], half_ref[...])


def last_norm_back(grad, sum_two, vec, turn):
    rows, width = grad.shape
    return pl.pallas_call(
        functools.partial(norm_kernel, tile=256),
        out_shape=[
            jax.ShapeDtypeStruct((rows, width), F32),
            jax.ShapeDtypeStruct((width, rows), BF),
            jax.ShapeDtypeStruct((8, width), F32),
        ],
        scratch_shapes=[pltpu.VMEM((rows, width), BF)],
        compiler_params=pltpu.CompilerParams(vmem_limit_bytes=40 * MB),
        cost_estimate=pl.CostEstimate(flops=2 * rows * width * width, bytes_accessed=14 * rows * width, transcendentals=0),
        name="last_norm_back",
    )(grad, sum_two, vec, turn)


def backward_kernel(
    grad_ref, half_t_ref, sum_one_ref, hidden_t_ref, mixed_t_ref, u_ref, e_ref, r_ref, out_ref, vec_ref,
    keep_ref, send_ref, one_ref, mixed_grad_ref, vec_grad_ref, bias_ref,
    two_ref, half_ref, act_ref, inner_ref, *, tile
):
    step = pl.program_id(0)
    rows, width = sum_one_ref.shape
    count = rows // tile
    cut = width // 2

    def rows_of(i):
        return pl.ds(pl.multiple_of(i * tile, tile), tile)

    @pl.when(step == 0)
    def _():
        two_ref[...] = grad_ref[...]
        half_ref[...] = to_half(grad_ref[...])

    bias_ref[...] = jnp.zeros_like(bias_ref)

    def body(i, carry):
        at = rows_of(i)
        act, slope = gelu_parts(u_ref[at, :])
        act_ref[at, :] = to_half(act)
        inner = to_half(mm(half_ref[at, :], r_ref[...]) * slope)
        inner_ref[at, :] = inner
        bias_ref[...] += column_sum(inner)
        two_ref[at, :] += mm_t(inner, e_ref[...])
        return carry

    lax.fori_loop(0, count, body, 0)
    block = u_ref.shape[1]
    steps = pl.num_programs(0)

    def set_grad(at, grad):
        at = pl.ds(pl.multiple_of(at, 128), grad.shape[1])
        keep_ref[:, at] = to_half(grad[:cut])
        send_ref[:, at] = to_half(grad[cut:])

    set_grad(step * block, mm(hidden_t_ref[...], inner_ref[...]))
    set_grad((step + steps) * block, mm(half_t_ref[...], act_ref[...]))

    @pl.when(step == pl.num_programs(0) - 1)
    def _():
        vec_grad_ref[...] = jnp.zeros_like(vec_grad_ref)

        def body(i, carry):
            at = rows_of(i)
            back, gain, shift = norm_back(sum_one_ref[at, :], vec_ref[3:4, :], two_ref[at, :])
            one_ref[at, :] = back
            half = to_half(back)
            half_ref[at, :] = half
            mixed_grad_ref[at, :] = to_half(mm_t(half, out_ref[...]))
            vec_grad_ref[0:1, :] += column_sum(back)
            vec_grad_ref[1:2, :] += gain
            vec_grad_ref[2:3, :] += shift
            return carry

        lax.fori_loop(0, count, body, 0)
        set_grad(2 * steps * block, mm(mixed_t_ref[...], half_ref[...]))


def feed_back(grad, half_t, sum_one, hidden_t, mixed_t, u, enc_mats, enc_ffn, vec):
    rows, width = sum_one.shape
    width_ff = u.shape[1]
    block = 640 if width_ff % 640 == 0 else width_ff
    steps = width_ff // block
    cut = width // 2
    whole = pl.BlockSpec((rows, width), lambda i: (0, 0))
    whole_t = pl.BlockSpec((width, rows), lambda i: (0, 0))
    grads = (cut, 2 * width_ff + width)
    return pl.pallas_call(
        functools.partial(backward_kernel, tile=256),
        grid=(steps,),
        in_specs=[
            whole,
            whole_t,
            whole,
            whole_t,
            whole_t,
            pl.BlockSpec((rows, block), lambda i: (0, i)),
            pl.BlockSpec((width, block), lambda i: (0, i)),
            pl.BlockSpec((width, block), lambda i: (0, i + steps)),
            pl.BlockSpec((width, width), lambda i: (0, 3)),
            pl.BlockSpec(vec.shape, lambda i: (0, 0)),
        ],
        out_specs=[pl.BlockSpec(grads, lambda i: (0, 0))] * 2
        + [
            whole,
            whole,
            pl.BlockSpec((8, width), lambda i: (0, 0)),
            pl.BlockSpec((1, block), lambda i: (0, i)),
        ],
        out_shape=[jax.ShapeDtypeStruct(grads, BF)] * 2
        + [
            jax.ShapeDtypeStruct((rows, width), F32),
            jax.ShapeDtypeStruct((rows, width), BF),
            jax.ShapeDtypeStruct((8, width), F32),
            jax.ShapeDtypeStruct((1, width_ff), F32),
        ],
        scratch_shapes=[
            pltpu.VMEM((rows, width), F32),
            pltpu.VMEM((rows, width), BF),
            pltpu.VMEM((rows, block), BF),
            pltpu.VMEM((rows, block), BF),
        ],
        compiler_params=pltpu.CompilerParams(vmem_limit_bytes=60 * MB),
        cost_estimate=pl.CostEstimate(
            flops=8 * rows * width * width_ff, bytes_accessed=6 * rows * width_ff, transcendentals=rows * width_ff
        ),
        name="feed_back",
    )(grad, half_t, sum_one, hidden_t, mixed_t, u, enc_ffn, enc_ffn, enc_mats, vec)


def attend_back_kernel(
    q_ref, k_ref, v_ref, o_ref, g_ref, log_ref, in_t_ref, x_t_ref, one_ref, wq_ref, wk_ref, wv_ref, *refs, chunk, first
):
    keep_ref, send_ref, grad_ref, vec_ref, kt_ref, dx_ref, dq_ref, dk_ref, dv_ref = refs[-9:]
    step_at = pl.program_id(0)
    width = x_t_ref.shape[0]
    cut = width // 2

    @pl.when(step_at == 0)
    def _():
        dx_ref[...] = one_ref[...]
        if first:
            keep_ref[...] = refs[0][...]
            send_ref[...] = refs[1][...]

    kt_ref[...] = k_ref[...].T
    dk_ref[...] = jnp.zeros_like(dk_ref)
    dv_ref[...] = jnp.zeros_like(dv_ref)

    def step(i, carry):
        at = pl.ds(i * chunk, chunk)
        query = q_ref[at, :] * BF(SCALE)
        grad = g_ref[at, :]
        cross = (grad.astype(F32) * o_ref[at, :].astype(F32)).T
        back = []
        for h in range(2):
            own, own_grad = own_lanes(query, h), own_lanes(grad, h)
            weighted = jnp.sum(cross[h * HDIM : (h + 1) * HDIM], axis=0, keepdims=True)
            probs = jnp.exp(mm_t(k_ref[...], own) - log_ref[0, pl.ds(h, 1), at])
            score_grad = to_half(probs * (mm_t(v_ref[...], own_grad) - weighted))
            dv_ref[...] += mm(to_half(probs), own_grad)
            dk_ref[...] += mm(score_grad, own)
            back.append(mm(kt_ref[...], score_grad))
        dq_ref[at, :] = to_half((join_rows(*back) * SCALE).T)
        return carry

    lax.fori_loop(0, q_ref.shape[0] // chunk, step, 0)
    dq = dq_ref[...]
    dk = to_half(dk_ref[...])
    dv = to_half(dv_ref[...])
    dx_ref[...] += mm_t(dq, wq_ref[...]) + mm_t(dk, wk_ref[...]) + mm_t(dv, wv_ref[...])
    for j, (left_ref, right) in enumerate(((in_t_ref, dq), (in_t_ref, dk), (x_t_ref, dv))):
        wgrad = to_half(mm(left_ref[...], right))
        at = pl.ds(pl.multiple_of(j * width + (first + step_at) * PAIR, PAIR), PAIR)
        keep_ref[:, at] = wgrad[:cut]
        send_ref[:, at] = wgrad[cut:]
    vec_ref[...] = jnp.zeros_like(vec_ref)
    vec_ref[0:1, :] = column_sum(dq)
    vec_ref[1:2, :] = column_sum(dv)

    @pl.when(step_at == pl.num_programs(0) - 1)
    def _():
        grad_ref[...] = dx_ref[...].astype(grad_ref.dtype)


def attend_back(query, keys, values, mixed, grad, log_total, in_t, x_t, so_far, enc_mats, part, parts, grads):
    rows, width = query.shape
    pairs = width // PAIR
    count = pairs // parts
    first = part * count
    cut = width // 2
    own = pl.BlockSpec((rows, PAIR), lambda i: (0, i + first))
    whole = pl.BlockSpec((rows, width), lambda i: (0, 0))
    whole_t = pl.BlockSpec((width, rows), lambda i: (0, 0))
    mats = [pl.BlockSpec((width, PAIR), lambda i, j=j: (0, i + first + j * pairs)) for j in range(3)]
    three = pl.BlockSpec((cut, 3 * width), lambda i: (0, 0))
    return pl.pallas_call(
        functools.partial(attend_back_kernel, chunk=256, first=first),
        grid=(count,),
        in_specs=[own] * 5
        + [pl.BlockSpec((1, 2, rows), lambda i: (i + first, 0, 0)), whole_t, whole_t, whole]
        + mats
        + [three] * len(grads),
        out_specs=[three, three, whole, pl.BlockSpec((8, PAIR), lambda i: (0, i))],
        out_shape=[jax.ShapeDtypeStruct((cut, 3 * width), BF)] * 2
        + [
            jax.ShapeDtypeStruct((rows, width), BF if part == parts - 1 else F32),
            jax.ShapeDtypeStruct((8, count * PAIR), F32),
        ],
        scratch_shapes=[
            pltpu.VMEM((PAIR, rows), BF),
            pltpu.VMEM((rows, width), F32),
            pltpu.VMEM((rows, PAIR), BF),
            pltpu.VMEM((rows, PAIR), F32),
            pltpu.VMEM((rows, PAIR), F32),
        ],
        compiler_params=pltpu.CompilerParams(vmem_limit_bytes=60 * MB),
        cost_estimate=pl.CostEstimate(
            flops=40 * rows * rows * width // parts, bytes_accessed=16 * rows * width, transcendentals=4 * rows * rows
        ),
        name="attend_back",
    )(query, keys, values, mixed, grad, log_total, in_t, x_t, so_far, enc_mats, enc_mats, enc_mats, *grads)


def heads_forward(query, key_ref, value_ref, prob_ref, n_keys):
    outs = []
    for pair in range(HEADS // 2):
        lanes = slice(pair * PAIR, (pair + 1) * PAIR)
        keys = key_ref[:, lanes]
        values_t = value_ref[:, lanes].T
        scaled = query[:, lanes] * BF(SCALE)
        mixed = []
        for h in range(2):
            scores = mm_t(keys, own_lanes(scaled, h))
            if n_keys < keys.shape[0]:
                row = lax.broadcasted_iota(jnp.int32, scores.shape, 0)
                scores = jnp.where(row < n_keys, scores, -jnp.inf)
            weights = jnp.exp(scores - jnp.max(scores, axis=0, keepdims=True))
            probs = weights * (1.0 / jnp.sum(weights, axis=0, keepdims=True))
            prob_ref[2 * pair + h] = probs
            mixed.append(mm(values_t, to_half(probs)))
        outs.append(to_half(join_rows(*mixed).T))
    return jnp.concatenate(outs, axis=1)


def heads_back(query, key_ref, value_ref, prob_ref, grad, dk_ref, dv_ref):
    outs = []
    for pair in range(HEADS // 2):
        lanes = slice(pair * PAIR, (pair + 1) * PAIR)
        keys_t = key_ref[:, lanes].T
        values = value_ref[:, lanes]
        scaled = query[:, lanes] * BF(SCALE)
        dk = dv = None
        back = []
        for h in range(2):
            own, own_grad = own_lanes(scaled, h), own_lanes(grad[:, lanes], h)
            probs = prob_ref[2 * pair + h]
            prob_grad = mm_t(values, own_grad)
            weighted = jnp.sum(probs * prob_grad, axis=0, keepdims=True)
            score_grad = to_half(probs * (prob_grad - weighted))
            back.append(mm(keys_t, score_grad))
            k_part, v_part = mm(score_grad, own), mm(to_half(probs), own_grad)
            dk = k_part if h == 0 else dk + k_part
            dv = v_part if h == 0 else dv + v_part
        dk_ref[:, lanes] = to_half(dk)
        dv_ref[:, lanes] = to_half(dv)
        outs.append(to_half((join_rows(*back) * SCALE).T))
    return jnp.concatenate(outs, axis=1)


def decode_kernel(
    x_ref, query_ref, target_ref, valid_ref, w_ref, head_ref, vec_ref, bias_ref, mem_ref, pos_ref, turn_ref,
    w_keep_ref, w_send_ref, f_keep_ref, f_send_ref, in_grad_ref, query_grad_ref, mem_grad_ref, vec_grad_ref, head_grad_ref, bias_grad_ref,
    mem_in, mem_half, cross_k, cross_v, cross_dk, cross_dv, cross_p,
    self_k, self_v, self_dk, self_dv, self_p, u_ref, act_ref, acc_ref, left_ref, *, n_steps, joints, block
):
    width = x_ref.shape[1]
    width_ff = u_ref.shape[1]
    blocks = width_ff // block
    first = 8 * width
    second = first + width_ff

    def mat(i):
        return w_ref[:, i * width : (i + 1) * width]

    cut = width // 2

    def left_of(values):
        return turned(turn_ref[...], values)

    def set_mat(i, left_t, right):
        grad = to_half(mm(left_t, right))
        w_keep_ref[:, i * width : (i + 1) * width] = grad[:cut]
        w_send_ref[:, i * width : (i + 1) * width] = grad[cut:]

    def set_ffn(at, left_t, right):
        grad = to_half(mm(left_t, right))
        f_keep_ref[:, at] = grad[:cut]
        f_send_ref[:, at] = grad[cut:]

    def vec(i):
        return vec_ref[i : i + 1, :]

    def set_vec(i, value):
        vec_grad_ref[i - 8 : i - 7, :] = value

    def lanes(i, start=0):
        return pl.ds(pl.multiple_of(start + i * block, 128), block)

    vec_grad_ref[...] = jnp.zeros_like(vec_grad_ref)
    x = x_ref[...]
    x_float = x.astype(F32)
    places = query_ref[...]
    self_in = to_half(x_float + places)
    self_q = to_half(mm(self_in, mat(0)) + vec(8))
    self_k[...] = to_half(mm(self_in, mat(1)))
    self_v[...] = to_half(mm(x, mat(2)) + vec(9))
    self_mixed = heads_forward(self_q, self_k, self_v, self_p, n_steps)
    sum_one = x_float + mm(self_mixed, mat(3)) + vec(10)
    one = layer_norm(sum_one, vec(11), vec(12))
    cross_in = to_half(one + places)
    cross_q = to_half(mm(cross_in, mat(4)) + vec(13))
    mem_in[...] = to_half(mem_ref[...] + pos_ref[...])
    mem_half[...] = to_half(mem_ref[...])
    cross_k[...] = to_half(mm(mem_in[...], mat(5)))
    cross_v[...] = to_half(mm(mem_half[...], mat(6)) + vec(14))
    cross_mixed = heads_forward(cross_q, cross_k, cross_v, cross_p, cross_k.shape[0])
    sum_two = one + mm(cross_mixed, mat(7)) + vec(15)
    two = layer_norm(sum_two, vec(16), vec(17))
    two_half = to_half(two)
    acc_ref[...] = two + vec(18)

    def forward(i, carry):
        u = mm(two_half, w_ref[:, lanes(i, first)]) + bias_ref[:, lanes(i)]
        u_ref[:, lanes(i)] = u
        acc_ref[...] += mm_t(to_half(gelu(u)), w_ref[:, lanes(i, second)])
        return carry

    lax.fori_loop(0, blocks, forward, 0)
    sum_three = acc_ref[...]
    three_half = to_half(layer_norm(sum_three, vec(19), vec(20)))
    error = mm_t(three_half, head_ref[...]) - target_ref[...]
    pred_grad = to_half(error * lax.rsqrt(error * error + 1.0) * valid_ref[...] / joints)
    head_grad_ref[...] = mm(pred_grad.T, three_half)
    sum_three_grad, gain, shift = norm_back(sum_three, vec(19), mm(pred_grad, head_ref[...]))
    set_vec(18, column_sum(sum_three_grad))
    set_vec(19, gain)
    set_vec(20, shift)
    out_grad = to_half(sum_three_grad)
    left_ref[0] = left_of(out_grad)
    left_ref[1] = left_of(two_half)
    acc_ref[...] = sum_three_grad

    def backward(i, carry):
        act, slope = gelu_parts(u_ref[:, lanes(i)])
        inner = to_half(mm(out_grad, w_ref[:, lanes(i, second)]) * slope)
        bias_grad_ref[:, lanes(i)] = column_sum(inner)
        acc_ref[...] += mm_t(inner, w_ref[:, lanes(i, first)])
        set_ffn(lanes(i), left_ref[1], inner)
        set_ffn(lanes(i, width_ff), left_ref[0], to_half(act))
        return carry

    lax.fori_loop(0, blocks, backward, 0)
    sum_two_grad, gain, shift = norm_back(sum_two, vec(16), acc_ref[...])
    set_vec(15, column_sum(sum_two_grad))
    set_vec(16, gain)
    set_vec(17, shift)
    out_grad = to_half(sum_two_grad)
    set_mat(7, left_of(cross_mixed), out_grad)
    mixed_grad = to_half(mm_t(out_grad, mat(7)))
    cross_dq = heads_back(cross_q, cross_k, cross_v, cross_p, mixed_grad, cross_dk, cross_dv)
    set_vec(13, column_sum(cross_dq))
    set_vec(14, column_sum(cross_dv[...]))
    mem_grad_ref[...] = mm_t(cross_dk[...], mat(5)) + mm_t(cross_dv[...], mat(6))
    set_mat(4, left_of(cross_in), cross_dq)
    set_mat(5, left_of(mem_in[...]), cross_dk[...])
    set_mat(6, left_of(mem_half[...]), cross_dv[...])
    cross_in_grad = mm_t(cross_dq, mat(4))
    sum_one_grad, gain, shift = norm_back(sum_one, vec(11), sum_two_grad + cross_in_grad)
    set_vec(10, column_sum(sum_one_grad))
    set_vec(11, gain)
    set_vec(12, shift)
    out_grad = to_half(sum_one_grad)
    set_mat(3, left_of(self_mixed), out_grad)
    mixed_grad = to_half(mm_t(out_grad, mat(3)))
    self_dq = heads_back(self_q, self_k, self_v, self_p, mixed_grad, self_dk, self_dv)
    set_vec(8, column_sum(self_dq))
    set_vec(9, column_sum(self_dv[...]))
    in_t = left_of(self_in)
    set_mat(0, in_t, self_dq)
    set_mat(1, in_t, self_dk[...])
    set_mat(2, left_of(x), self_dv[...])
    self_in_grad = mm_t(self_dq, mat(0)) + mm_t(self_dk[...], mat(1))
    in_grad_ref[...] = to_half(sum_one_grad + self_in_grad + mm_t(self_dv[...], mat(2)))
    query_grad_ref[...] = self_in_grad + cross_in_grad


def decode(x, places, target, valid, weights, head_t, vec, bias, memory, positions, turn, n_steps, joints):
    rows, width = x.shape
    mem_rows = memory.shape[0]
    width_ff = bias.shape[1]
    half = lambda n: pltpu.VMEM((n, width), BF)
    return pl.pallas_call(
        functools.partial(
            decode_kernel, n_steps=n_steps, joints=joints, block=640 if width_ff % 640 == 0 else width_ff
        ),
        out_shape=[
            jax.ShapeDtypeStruct((width // 2, 8 * width), BF),
            jax.ShapeDtypeStruct((width // 2, 8 * width), BF),
            jax.ShapeDtypeStruct((width // 2, 2 * width_ff), BF),
            jax.ShapeDtypeStruct((width // 2, 2 * width_ff), BF),
            jax.ShapeDtypeStruct((rows, width), BF),
            jax.ShapeDtypeStruct((rows, width), F32),
            jax.ShapeDtypeStruct((mem_rows, width), F32),
            jax.ShapeDtypeStruct((16, width), F32),
            jax.ShapeDtypeStruct(head_t.shape, F32),
            jax.ShapeDtypeStruct((1, width_ff), F32),
        ],
        scratch_shapes=[half(mem_rows)] * 6
        + [pltpu.VMEM((HEADS, mem_rows, rows), F32)]
        + [half(rows)] * 4
        + [
            pltpu.VMEM((HEADS, rows, rows), F32),
            pltpu.VMEM((rows, width_ff), F32),
            pltpu.VMEM((rows, width_ff), BF),
            pltpu.VMEM((rows, width), F32),
            pltpu.VMEM((2, width, rows), BF),
        ],
        compiler_params=pltpu.CompilerParams(vmem_limit_bytes=60 * MB),
        cost_estimate=pl.CostEstimate(
            flops=12 * mem_rows * width * width, bytes_accessed=4 * weights.size, transcendentals=rows * width_ff
        ),
        name="decode",
    )(x, places, target, valid, weights, head_t, vec, bias, memory, positions, turn)


def adamw(weight, gradient, moment_one, moment_two, step_rate):
    moment_one = beta_first * moment_one + (1.0 - beta_first) * gradient
    moment_two = beta_second * moment_two + (1.0 - beta_second) * gradient * gradient
    mean_hat = moment_one / (1.0 - beta_first**STEP)
    square_hat = moment_two / (1.0 - beta_second**STEP)
    updated = weight - step_rate * (
        mean_hat / (jnp.sqrt(square_hat) + epsilon) + decay_rate * weight
    )
    return (moment_one, moment_two, updated, updated.astype(BF))


def update_kernel(*refs, rates):
    count = len(rates)
    ins, outs = refs[: 4 * count], refs[4 * count :]
    for i, rate in enumerate(rates):
        values = adamw(*(ref[...] for ref in ins[4 * i : 4 * i + 4]), rate)
        for ref, value in zip(outs[4 * i : 4 * i + 4], values):
            ref[...] = value


def update(groups, rates):
    shapes = []
    for group in groups:
        shapes += [jax.ShapeDtypeStruct(group[0].shape, F32)] * 3
        shapes.append(jax.ShapeDtypeStruct(group[0].shape, BF))
    outs = pl.pallas_call(
        functools.partial(update_kernel, rates=rates),
        out_shape=shapes,
        compiler_params=pltpu.CompilerParams(vmem_limit_bytes=56 * MB),
        name="update",
    )(*(array for group in groups for array in group))
    return [outs[4 * i : 4 * i + 4] for i in range(len(groups))]


def pad_to(values, rows, columns):
    return jnp.pad(values, ((0, rows - values.shape[0]), (0, columns - values.shape[1])))


def side_by_side(mats):
    return jnp.concatenate([mats[i] for i in range(mats.shape[0])], axis=1)


def gather(columns):
    return lax.all_gather(columns, ALL, axis=0, tiled=True)


def width_bits(axis):
    return (lax.axis_size(axis) - 1).bit_length()


def bit_groups():
    low = width_bits("seq")
    others = list(range(low + width_bits("dp") - 1, low, -1))
    seq = list(range(low - 1, -1, -1))
    groups = [[low]]
    for bits in (others, seq):
        groups += [bits[i : i + 2] for i in range(0, len(bits), 2)]
    return groups


def spread(bits, place):
    return sum(((place >> k) & 1) << bit for k, bit in enumerate(reversed(bits)))


def turn_matrix(width):
    order = [bit for bits in bit_groups() for bit in bits]
    devices = 1 << len(order)
    relative = np.array([spread(order, j) for j in range(devices)], np.int32)
    shard = width // devices
    source = jnp.bitwise_xor(jnp.asarray(relative), lax.axis_index(ALL).astype(jnp.int32))
    source = (source[:, None] * shard + jnp.arange(shard, dtype=jnp.int32)[None, :]).reshape(width)
    return (source[:, None] == jnp.arange(width, dtype=jnp.int32)[None, :]).astype(BF)


def exchange(values, distance):
    low = width_bits("seq")
    axis, distance = ("dp", distance >> low) if distance >> low else ("seq", distance)
    pairs = [(i, i ^ distance) for i in range(lax.axis_size(axis))]
    return lax.ppermute(values, axis, pairs)


class Sum:
    def __init__(self, blocks):
        self.blocks = list(blocks)
        self.groups = bit_groups()
        self.arrived = None

    def start(self):
        bits = self.groups.pop(0)
        self.arrived = [exchange(block, spread(bits, j)) for j, block in enumerate(self.blocks) if j]

    def add(self):
        arrays = [self.blocks[0]] + self.arrived
        count = 1 << len(self.groups[0]) if self.groups else 1
        rows = arrays[0].shape[-2] // count
        totals = []
        for j in range(count):
            parts = [array[..., j * rows : (j + 1) * rows, :].astype(F32) for array in arrays]
            total = functools.reduce(jnp.add, parts)
            totals.append(to_half(total) if self.groups else total)
        self.blocks = totals
        self.arrived = None

    def step(self):
        self.add()
        if self.groups:
            self.start()

    def finish(self):
        while self.groups or self.arrived is not None:
            if self.arrived is None:
                self.start()
            self.step()
        return self.blocks[0]


class Swap:
    def __init__(self, pieces):
        self.pieces = list(pieces)

    def start(self):
        self.arrived = [exchange(piece, j) for j, piece in enumerate(self.pieces) if j]

    def result(self):
        return [self.pieces[0]] + self.arrived


def by_rank(pieces):
    me = lax.axis_index("seq")
    return [lax.dynamic_index_in_dim(pieces, me ^ i, 0, keepdims=False) for i in range(pieces.shape[0])]


def tie(values, *sums):
    values, arrived = lax.optimization_barrier((values, [s.arrived for s in sums]))
    for s, a in zip(sums, arrived):
        s.arrived = a
    return values


def per_device(
    enc_input,
    dec_input,
    targets,
    lengths,
    attention_mats,
    expand_mats,
    reduce_mats,
    action_head,
    query_pos,
    vectors,
    expand_bias,
    *moments,
):
    ranks = lax.axis_size("seq")
    seq_index = lax.axis_index("seq")
    items, enc_part, width = enc_input.shape
    dec_part = dec_input.shape[1]
    joints = targets.shape[2]
    width_ff = expand_mats.shape[2]
    shard = attention_mats.shape[1]
    bias_part = expand_bias.shape[0]
    n_query, n_vec = query_pos.shape[0], vectors.shape[0]
    vec_at = (n_query + 7) // 8 * 8
    head_at = (vec_at + n_vec + 7) // 8 * 8
    n_small = (head_at + joints + 127) // 128 * 128
    devices = width // shard
    dec_rows = (n_query + 127) // 128 * 128

    reduce_t = jnp.swapaxes(reduce_mats, 1, 2)
    half_mats = to_half(attention_mats)
    half_expand = to_half(expand_mats)
    half_reduce = to_half(reduce_t)
    small_local = to_half(
        jnp.concatenate(
            [
                pad_to(query_pos.T, shard, vec_at),
                pad_to(vectors.T, shard, head_at - vec_at),
                pad_to(action_head, shard, n_small - head_at),
            ],
            axis=1,
        )
    )
    bias_local = to_half(jnp.pad(expand_bias, (0, shard * 128 - bias_part)).reshape(shard, 128))
    enc_all = gather(
        jnp.concatenate(
            [side_by_side(half_mats[0:4]), small_local, bias_local, half_expand[0], half_reduce[0]],
            axis=1,
        )
    )
    dec_all = gather(
        jnp.concatenate([side_by_side(half_mats[4:12]), half_expand[1], half_reduce[1]], axis=1)
    )

    assert items == ranks

    def swapped(pieces):
        swap = Swap(by_rank(pieces))
        swap.start()
        return swap.result()

    enc_x = jnp.concatenate(swapped(enc_input))
    dec_x = jnp.concatenate(by_rank(jnp.stack(swapped(dec_input))))
    dec_x = pad_to(dec_x, dec_rows, width)
    target = jnp.concatenate(by_rank(jnp.stack(swapped(targets))))
    target = pad_to(target, dec_rows, 128)
    turn = turn_matrix(width)
    table = sine_table(ranks * enc_part, width).reshape(ranks, enc_part, width)
    positions = jnp.concatenate(by_rank(jnp.asarray(table)))
    length = lengths[seq_index]
    valid = jnp.broadcast_to((jnp.arange(dec_rows) < length).astype(F32)[:, None], (dec_rows, 128))

    at = 4 * width
    enc_att = enc_all[:, :at]
    enc_ffn = enc_all[:, at + n_small + 128 :]
    small = enc_all[:, at : at + n_small].T
    bias_all = enc_all[:, at + n_small : at + n_small + 128].reshape(devices, shard * 128)
    bias_all = bias_all[:, :bias_part].reshape(1, 2 * width_ff).astype(F32)
    query_whole = pad_to(small[:n_query].astype(F32), dec_rows, width)
    vec = pad_to(small[vec_at : vec_at + n_vec].astype(F32), (n_vec + 7) // 8 * 8, width)
    head_t = pad_to(small[head_at : head_at + joints], 128, width)
    query, keys, values, mixed, log_total = attend(enc_x, positions, enc_att, vec)
    sum_one, hidden, u, sum_two, memory = feed_forward(
        mixed, enc_x, enc_att, vec, enc_ffn, bias_all[:, :width_ff]
    )
    memory, in_t, x_t, mixed_t, hidden_t = lax.optimization_barrier(
        (memory, *lefts(enc_x, positions, mixed, hidden, turn))
    )
    (
        w_keep, w_send, f_keep, f_send,
        dec_in_grad, query_grad, memory_grad, dec_vec_grads, head_grad_t, dec_bias_grad,
    ) = decode(
        dec_x, query_whole, target, valid, dec_all, head_t, vec, bias_all[:, width_ff:], memory, positions, turn,
        n_query, joints,
    )
    dec_ffn, dec_att = Sum([f_keep, f_send]), Sum([w_keep, w_send])
    dec_ffn.start()
    dec_att.start()
    two_grad, half_t, vec_grads_c = tie(last_norm_back(memory_grad, sum_two, vec, turn), dec_ffn, dec_att)
    dec_ffn.step()
    dec_swap = Swap(by_rank(dec_in_grad[:n_query].reshape(ranks, dec_part, width)))
    keep, send, one_grad, mixed_grad, vec_grads_b, enc_bias_grad, att_held = tie(
        [
            *feed_back(two_grad, half_t, sum_one, hidden_t, mixed_t, u, enc_att, enc_ffn, vec),
            (dec_att.blocks, dec_att.arrived),
        ],
        dec_ffn,
    )
    dec_att.blocks, dec_att.arrived = att_held
    dec_swap.start()
    enc_ffn_sum = Sum([keep, send])
    enc_ffn_sum.start()
    dec_ffn.step()
    dec_att.step()

    def back(so_far, part, grads):
        return attend_back(
            query, keys, values, mixed, mixed_grad, log_total, in_t, x_t, so_far, enc_att, part, 2, grads
        )

    keep, send, so_far, vec_grads_d = tie(back(one_grad, 0, ()), dec_ffn, dec_att, enc_ffn_sum)
    dec_ffn.step()
    dec_att.step()
    enc_ffn_sum.step()
    dec_grad = jnp.stack(by_rank(jnp.stack(dec_swap.result())))
    vec_grads = jnp.concatenate([vec_grads_b[:3], vec_grads_c[:3], dec_vec_grads[: n_vec - 8]])
    small_rows = jnp.concatenate(
        [
            pad_to(query_grad[:n_query], vec_at + 2, width),
            pad_to(vec_grads, head_at - vec_at - 2, width),
            pad_to(head_grad_t[:joints], n_small - head_at, width),
        ]
    )
    bias_grad = jnp.concatenate([enc_bias_grad, dec_bias_grad], axis=1).reshape(devices, bias_part)
    bias_grad = pad_to(bias_grad, devices, shard * 128).reshape(width, 128)
    small_grad = to_half(
        jnp.concatenate([mm_t(turn, to_half(small_rows)), mm(turn, to_half(bias_grad))], axis=1)
    )
    keep, send, enc_grad, vec_grads_e, small_grad = tie([*back(so_far, 1, (keep, send)), small_grad], dec_att)
    dec_att_total = dec_att.finish()
    late_rows = jnp.concatenate([vec_grads_d[:2], vec_grads_e[:2]], axis=1)
    late_grad = to_half(mm_t(turn, to_half(pad_to(late_rows, 128, width))))
    half = width // 2
    last = Sum(
        [
            jnp.concatenate([keep, small_grad[:half], late_grad[:half]], axis=1),
            jnp.concatenate([send, small_grad[half:], late_grad[half:]], axis=1),
        ]
    )
    last.start()
    enc_grad = tie(enc_grad, enc_ffn_sum, last)
    last.step()
    enc_ffn_sum.step()
    grad_swap = Swap([enc_grad[j * enc_part : (j + 1) * enc_part] for j in range(ranks)])
    grad_swap.start()
    dec_ffn_total = tie(dec_ffn.finish(), last, enc_ffn_sum)
    last.step()
    enc_ffn_total, last_total = enc_ffn_sum.finish(), last.finish()
    outputs = [jnp.stack(by_rank(jnp.stack(grad_swap.result()))), dec_grad]

    small_total = last_total[:, 3 * width :]
    gradients = (
        jnp.stack(
            [last_total[:, i * width : (i + 1) * width] for i in range(3)]
            + [enc_ffn_total[:, 2 * width_ff :]]
            + [dec_att_total[:, i * width : (i + 1) * width] for i in range(8)]
        ),
        jnp.stack([enc_ffn_total[:, :width_ff], dec_ffn_total[:, :width_ff]]),
        jnp.stack([enc_ffn_total[:, width_ff : 2 * width_ff], dec_ffn_total[:, width_ff:]]),
        small_total[:, head_at : head_at + joints],
        small_total[:, :n_query],
        jnp.concatenate(
            [small_total[:, n_small + 128 : n_small + 130], small_total[:, vec_at + 2 : vec_at + n_vec]], axis=1
        ),
        small_total[:, n_small : n_small + 128].reshape(1, -1)[:, :bias_part],
    )

    def views(mats, expand, reduce, head, query, vector, bias):
        return (mats, expand, jnp.swapaxes(reduce, 1, 2), head, query.T, vector.T, bias.reshape(1, -1))

    weights = views(attention_mats, expand_mats, reduce_mats, action_head, query_pos, vectors, expand_bias)
    firsts, seconds = views(*moments[:7]), views(*moments[7:])
    rates = (rate_matrix,) * 4 + (rate_vector,) * 3
    for i, results in enumerate(update(list(zip(weights, gradients, firsts, seconds)), rates)):
        if i == 2:
            results = [jnp.swapaxes(value, 1, 2) for value in results]
        if i in (4, 5):
            results = [value.T for value in results]
        if i == 6:
            results = [value.reshape(-1) for value in results]
        outputs.extend(results)
    return tuple(outputs)


def solution(mesh):
    rows = P("dp", "seq", None)
    weight_specs = (
        P(None, ALL, None),
        P(None, ALL, None),
        P(None, None, ALL),
        P(ALL, None),
        P(None, ALL),
        P(None, ALL),
        P(ALL),
    )
    in_specs = (rows, rows, rows, P("dp")) + weight_specs * 3
    out_specs = (rows, rows) + tuple(spec for spec in weight_specs for unused in range(4))
    return jax.shard_map(
        per_device, mesh=mesh, in_specs=in_specs, out_specs=out_specs, check_vma=False
    )
```

time: 857 us -> 472 us (0.55)
  waiting for transfers between devices: 431 us -> 112 us
  matrix products: 203 us -> 2.93 us
  Pallas kernels: 53.4 us -> 181 us
  starting transfers between devices: 19.3 us -> 58.7 us
  local copies, waits for them, and re-layouts: 76.1 us -> 53.7 us
  blocking collectives: 10.6 us -> 0 us
    reduce_scatter x2 -> x0, waiting for transfers between devices: 284 us -> none  [scatter(): lax.psum_scatter(columns, ALL, scatter_dimension=0, tiled=True).astype(F32)]
    pallas_call x1 -> x8, Pallas kernels: 26.6 us -> 147 us  [the longest x2 42 us: attend_back(): pl.pallas_call(functools.partial(attend_back_kernel, chunk=256, first=fir...]
    dot_general x27 -> x0, matrix products: 97 us -> none  [the longest x17 55.3 us: t_mm(): lax.dot_general(a, b, (((0,), (0,)), ((), ())), preferred_element_type=F32)]
    ppermute x0 -> x43, waiting for transfers between devices: none -> 89.7 us  [exchange(): return lax.ppermute(values, axis, pairs)]
    all_to_all x4 -> x0, waiting for transfers between devices: 81.4 us -> none  [the longest x2 45.6 us: to_parts(): lax.all_to_all(values.reshape(per_rank, ranks * part, width), 'seq', 1, 0...]
    ppermute x0 -> x43, starting transfers between devices: none -> 58.6 us  [exchange(): return lax.ppermute(values, axis, pairs)]
    dot_general x17 -> x1, matrix products: 52.3 us -> 1.26 us  [mm(): lax.dot_general(a, b, (((1,), (0,)), ((), ())), preferred_element_type=F32)]
    dot_general x17 -> x2, matrix products: 46.4 us -> 1.68 us  [mm_t(): lax.dot_general(a, b, (((1,), (1,)), ((), ())), preferred_element_type=F32)]
  transfers between devices with their start and end apart: 8 -> 45, of which waited for: 7 -> 15; matrix products, arithmetic and copies ran while one was open for 10% -> 16% of each run, Pallas kernels for 3% -> 30%
where the time goes in v2:
time: 472 us; the launch traced here: 467 us
  Pallas kernels  181 us (38%)
  waiting for transfers between devices  112 us (24%)
  starting transfers between devices  58.7 us (12%)
  local copies, waits for them, and re-layouts  53.7 us (11%)
  other arithmetic  44.2 us (9%)
  between operations  15.1 us (3%)
    ppermute x43, waiting for transfers between devices, exchange(): return lax.ppermute(values, axis, pairs)  89.7 us
    ppermute x43, starting transfers between devices, exchange(): return lax.ppermute(values, axis, pairs)  58.6 us
    pallas_call x2, Pallas kernels, attend_back(): pl.pallas_call(functools.partial(attend_back_kernel, chunk=256, first=fir...  42 us
    pallas_call x1, Pallas kernels, feed_back(): pl.pallas_call(functools.partial(backward_kernel, tile=256), grid=(steps,...  37.7 us
    pallas_call x1, Pallas kernels, decode(): pl.pallas_call(functools.partial(decode_kernel, n_steps=n_steps, joints=j...  35.1 us
    pallas_call x1, Pallas kernels, attend(): pl.pallas_call(functools.partial(attend_kernel, chunk=256), grid=(pairs,)...  33.4 us
    unnamed x102, local copies, waits for them, and re-layouts  23.4 us
    pallas_call x1, Pallas kernels, feed_forward(): pl.pallas_call(functools.partial(forward_kernel, tile=256), grid=(steps,)...  23.2 us
  transfers between devices with their start and end apart: 45, of which 15 were waited for; matrix products, arithmetic and copies ran while one was open for 16% of the time, Pallas kernels for 30%

profile of v2, /device:TPU:0, one launch (start us, length us, event | category | flops | bytes accessed | tf_op | source)
XLA Modules:
  0.0 467.4 jit_solution(13461162072743979655)
XLA Ops:
  28.4 5.1 %collective-permute-start.8 = (f32[25,14]{0,1:T(8,128)}, f32[25,14]{0,1:T(8,128)}, u32[]{:S(2)}, u32[]{:S(2)}) collective-permute-start(f32[25,14]{0,1:T(8,128)} %bitcast.212), channel_id=1, source_target_pairs={{0,3},{1,2},{2,1},{3,0},{4,7},{5,6},{6,5},{7,4},{8,11},{9,10},{10,... | collective-permute-start | bytes 4208 | tf_op jit(solution)/shard_map/ppermute | solution.py:782
  37.2 3.8 collective-permute-start.5
  49.4 2.3 collective-permute-start.2
  55.4 10.4 %collective-permute-done = bf16[256,512]{1,0:T(8,128)(2,1)S(1)} collective-permute-done((bf16[256,512]{1,0:T(8,128)(2,1)}, bf16[256,512]{1,0:T(8,128)(2,1)S(1)}, u32[]{:S(2)}, u32[]{:S(2)}) %collective-permute-start) | collective-permute-done | bytes 262176 | tf_op jit(solution)/shard_map/ppermute | solution.py:782
  65.8 7.5 %collective-permute-done.2 = bf16[256,512]{1,0:T(8,128)(2,1)S(1)} collective-permute-done((bf16[256,512]{1,0:T(8,128)(2,1)}, bf16[256,512]{1,0:T(8,128)(2,1)S(1)}, u32[]{:S(2)}, u32[]{:S(2)}) %collective-permute-start.2) | collective-permute-done | bytes 262176 | tf_op jit(solution)/shard_map/ppermute | solution.py:782
  73.3 24.9 %collective-permute-done.1 = bf16[256,512]{1,0:T(8,128)(2,1)S(1)} collective-permute-done((bf16[256,512]{1,0:T(8,128)(2,1)S(1)}, bf16[256,512]{1,0:T(8,128)(2,1)S(1)}, u32[]{:S(2)}, u32[]{:S(2)}) %collective-permute-start.1) | collective-permute-done | bytes 262176 | tf_op jit(solution)/shard_map/ppermute | solution.py:782
  99.3 10.6 %all-gather.3.cloned.1.call-done = bf16[512,8832]{1,0:T(8,128)(2,1)} async-done(((bf16[16,8832]{1,0:T(8,128)(2,1)}), bf16[512,8832]{1,0:T(8,128)(2,1)}) %all-gather.3.cloned.1.call-update) | async-done | bytes 9043984 | tf_op jit(solution)/shard_map/all_gather | solution.py:747
  114.5 3.2 slice.671.wq_ref.wk_ref.wv_ref.out_ref
  117.7 6.2 %slice.689.e_ref.r_ref = bf16[512,6400]{1,0:T(8,128)(2,1)} slice(bf16[512,8832]{1,0:T(8,128)(2,1)} %all-gather.3.cloned.1.call-done), slice={[0:512], [2432:8832]} | slice | bytes 13107200 | tf_op jit(solution)/shard_map/slice | solution.py:917
  123.8 33.4 %attend.1 = (bf16[1024,512]{1,0:T(8,128)(2,1)}, bf16[1024,512]{1,0:T(8,128)(2,1)}, bf16[1024,512]{1,0:T(8,128)(2,1)}, bf16[1024,512]{1,0:T(8,128)(2,1)}, f32[4,2,1024]{2,1,0:T(2,128)}) custom-call(bf16[1024,512]{1,0:T(8,128)(2,1)} %pad_maximum_fusion.1.x_ref, f32[1024,512]{1,0:T(8,128)} %pad_maximum_fusion.pos_ref, ...), custom_call_target="tpu_custom_call" | custom-call | flops 8589934592 | bytes 6291456 | tf_op jit(solution)/shard_map/attend/pallas_call | solution.py:137
  157.8 23.2 %feed_forward.1 = (f32[1024,512]{1,0:T(8,128)}, bf16[1024,512]{1,0:T(8,128)(2,1)}, f32[1024,3200]{1,0:T(8,128)}, f32[1024,512]{1,0:T(8,128)}, f32[1024,512]{1,0:T(8,128)}) custom-call(bf16[1024,512]{1,0:T(8,128)(2,1)} %get-tuple-element.154.mixed_ref.o_ref, bf16[1024,512]{1,0:T(8,128)(2,1)} %pad_maximum_fusion.1.x_ref, ...), custom_call_target="tpu_custom_call" | custom-call | flops 6710886400 | bytes 13107200 | tf_op jit(solution)/shard_map/feed_forward/pallas_call | solution.py:201
  182.4 2.4 lefts.1
  188.7 11.7 %all-gather.5.cloned.1.call-done.w_ref = bf16[512,10496]{1,0:T(8,128)(2,1)} async-done(((bf16[16,10496]{1,0:T(8,128)(2,1)}), bf16[512,10496]{1,0:T(8,128)(2,1)}) %all-gather.5.cloned.1.call-update) | async-done | bytes 10747920 | tf_op jit(solution)/shard_map/all_gather | solution.py:747
  201.1 35.1 %decode.1 = (bf16[256,4096]{1,0:T(8,128)(2,1)}, bf16[256,4096]{1,0:T(8,128)(2,1)}, bf16[256,6400]{1,0:T(8,128)(2,1)}, bf16[256,6400]{1,0:T(8,128)(2,1)}, bf16[12...) custom-call(bf16[128,512]{1,0:T(8,128)(2,1)} %fusion.17.x_ref, ...), custom_call_target="tpu_custom_call" | custom-call | flops 3221225472 | bytes 21495808 | tf_op jit(solution)/shard_map/decode/pallas_call | solution.py:670
  248.7 2.4 last_norm_back.1
  252.7 3.5 add_convert_fusion.4
  259.7 37.7 %feed_back.1 = (bf16[256,6912]{1,0:T(8,128)(2,1)}, bf16[256,6912]{1,0:T(8,128)(2,1)}, f32[1024,512]{1,0:T(8,128)}, bf16[1024,512]{1,0:T(8,128)(2,1)}, f32[8,512]{1,0:T(8,128)}, /*index=5*/f32[1,3200]{1,0:T(1,128)}) custom-call(f32[1024,512]{1,0:T(8,128)} %copy-done.7, bf16[512,1024]{1,0:T(8,128)(2,1)} %copy-done.8, ...), custom_call_target="tpu_custom_call" | custom-call | flops 13421772800 | bytes 19660800 | tf_op jit(solution)/shard_map/feed_back/pallas_call | solution.py:355
  299.4 2.8 add_convert_fusion.21
  303.9 3.8 add_convert_fusion.8
  310.5 20.8 %attend_back.2 = (bf16[256,1536]{1,0:T(8,128)(2,1)}, bf16[256,1536]{1,0:T(8,128)(2,1)}, f32[1024,512]{1,0:T(8,128)}, f32[8,256]{1,0:T(8,128)}) custom-call(bf16[1024,512]{1,0:T(8,128)(2,1)} %get-tuple-element.151.q_ref, bf16[1024,512]{1,0:T(8,128)(2,1)} %get-tuple-element.152.k_ref, bf16[1024,512]{1,0:T(8,128)(2,1)} %get-tuple-element.153.v_ref, ...), custom_call_target="tpu_custom_call" | custom-call | flops 10737418240 | bytes 8388608 | tf_op jit(solution)/shard_map/attend_back/pallas_call | solution.py:464
  334.3 2.7 collective-permute-start.14
  339.1 2.4 collective-permute-done.14
  341.5 3.5 collective-permute-done.17
  352.4 2.4 add_convert_fusion
  358.5 21.2 %attend_back.3 = (bf16[256,1536]{1,0:T(8,128)(2,1)}, bf16[256,1536]{1,0:T(8,128)(2,1)}, bf16[1024,512]{1,0:T(8,128)(2,1)}, f32[8,256]{1,0:T(8,128)}) custom-call(bf16[1024,512]{1,0:T(8,128)(2,1)} %get-tuple-element.151.q_ref, bf16[1024,512]{1,0:T(8,128)(2,1)} %get-tuple-element.152.k_ref, bf16[1024,512]{1,0:T(8,128)(2,1)} %get-tuple-element.153.v_ref, ...), custom_call_target="tpu_custom_call" | custom-call | flops 10737418240 | bytes 8388608 | tf_op jit(solution)/shard_map/attend_back/pallas_call | solution.py:464
  384.7 9.6 %collective-permute-done.25 = bf16[64,6912]{1,0:T(8,128)(2,1)} collective-permute-done((bf16[64,6912]{1,0:T(8,128)(2,1)}, bf16[64,6912]{1,0:T(8,128)(2,1)}, u32[]{:S(2)}, u32[]{:S(2)}) %collective-permute-start.25) | collective-permute-done | bytes 884768 | tf_op jit(solution)/shard_map/ppermute | solution.py:782
  394.3 5.3 %collective-permute-done.24 = bf16[64,6912]{1,0:T(8,128)(2,1)S(1)} collective-permute-done((bf16[64,6912]{1,0:T(8,128)(2,1)}, bf16[64,6912]{1,0:T(8,128)(2,1)S(1)}, u32[]{:S(2)}, u32[]{:S(2)}) %collective-permute-start.24) | collective-permute-done | bytes 884768 | tf_op jit(solution)/shard_map/ppermute | solution.py:782
  409.8 12.5 %collective-permute-done.39 = bf16[16,6912]{1,0:T(8,128)(2,1)S(1)} collective-permute-done((bf16[16,6912]{1,0:T(8,128)(2,1)S(1)}, bf16[16,6912]{1,0:T(8,128)(2,1)S(1)}, u32[]{:S(2)}, u32[]{:S(2)}) %collective-permute-start.39) | collective-permute-done | bytes 221216 | tf_op jit(solution)/shard_map/ppermute | solution.py:782
  424.1 3.8 collective-permute-done.29
  427.9 5.8 %collective-permute-start.38 = (bf16[16,6912]{1,0:T(8,128)(2,1)S(1)}, bf16[16,6912]{1,0:T(8,128)(2,1)S(1)}, u32[]{:S(2)}, u32[]{:S(2)}) collective-permute-start(bf16[16,6912]{1,0:T(8,128)(2,1)S(1)} %get-tuple-element.375), channel_id=1, source_target_pairs={{0,2},{1,3},{2,0},{3,1},{4,6},{5,7},{6,4},{7,5},{8,10},{9,11},{10,... | collective-permute-start | bytes 663560 | tf_op jit(solution)/shard_map/ppermute | solution.py:782
  434.0 7.7 %collective-permute-done.38 = bf16[16,6912]{1,0:T(8,128)(2,1)S(1)} collective-permute-done((bf16[16,6912]{1,0:T(8,128)(2,1)S(1)}, bf16[16,6912]{1,0:T(8,128)(2,1)S(1)}, u32[]{:S(2)}, u32[]{:S(2)}) %collective-permute-start.38) | collective-permute-done | bytes 221216 | tf_op jit(solution)/shard_map/ppermute | solution.py:782
  454.5 4.7 %update.1 = (f32[12,16,512]{2,1,0:T(8,128)}, f32[12,16,512]{2,1,0:T(8,128)}, f32[12,16,512]{2,1,0:T(8,128)}, bf16[12,16,512]{2,1,0:T(8,128)(2,1)}, f32[2,16,3200...) custom-call(f32[12,16,512]{2,1,0:T(8,128)} %refs_0_.1, ...), custom_call_target="tpu_custom_call" | custom-call | tf_op jit(solution)/shard_map/update/pallas_call | solution.py:729
  (279 shorter events, 120.0 us)
Async XLA Ops:
  7.2 102.7 %all-gather.3.cloned.1.call-start = ((), (), s32[]{:S(2)}) async-start(), calls=%async_computation | async-start | bytes 9326592 | tf_op jit(solution)/shard_map/all_gather | solution.py:747
  14.8 185.6 %all-gather.5.cloned.1.call-start = ((), (), s32[]{:S(2)}) async-start(), calls=%async_computation.1 | async-start | bytes 11083776 | tf_op jit(solution)/shard_map/all_gather | solution.py:747
  28.4 18.8 %collective-permute-start.8 = (f32[25,14]{0,1:T(8,128)}, f32[25,14]{0,1:T(8,128)}, u32[]{:S(2)}, u32[]{:S(2)}) collective-permute-start(f32[25,14]{0,1:T(8,128)} %bitcast.212), channel_id=1, source_target_pairs={{0,3},{1,2},{2,1},{3,0},{4,7},{5,6},{6,5},{7,4},{8,11},{9,10},{10,... | collective-permute-start | bytes 4208 | tf_op jit(solution)/shard_map/ppermute | solution.py:782
  34.7 14.8 %collective-permute-start.7 = (f32[25,14]{0,1:T(8,128)}, f32[25,14]{0,1:T(8,128)}, u32[]{:S(2)}, u32[]{:S(2)}) collective-permute-start(f32[25,14]{0,1:T(8,128)} %bitcast.213), channel_id=1, source_target_pairs={{0,2},{1,3},{2,0},{3,1},{4,6},{5,7},{6,4},{7,5},{8,10},{9,11},{10,... | collective-permute-start | bytes 4208 | tf_op jit(solution)/shard_map/ppermute | solution.py:782
  37.2 16.2 %collective-permute-start.5 = (bf16[25,512]{1,0:T(8,128)(2,1)}, bf16[25,512]{1,0:T(8,128)(2,1)}, u32[]{:S(2)}, u32[]{:S(2)}) collective-permute-start(bf16[25,512]{1,0:T(8,128)(2,1)} %bitcast.209), channel_id=1, source_target_pairs={{0,3},{1,2},{2,1},{3,0},{4,7},{5,6},{6,5},{7,4},{8,11},{9,10},{10,... | collective-permute-start | bytes 76808 | tf_op jit(solution)/shard_map/ppermute | solution.py:782
  47.9 17.9 %collective-permute-start = (bf16[256,512]{1,0:T(8,128)(2,1)}, bf16[256,512]{1,0:T(8,128)(2,1)S(1)}, u32[]{:S(2)}, u32[]{:S(2)}) collective-permute-start(bf16[256,512]{1,0:T(8,128)(2,1)} %get-tuple-element.403), channel_id=1, source_target_pairs={{0,1},{1,0},{2,3},{3,2},{4,5},{5,4},{6,7},{7,6},{8,9},{9,8},{10,11... | collective-permute-start | bytes 786440 | tf_op jit(solution)/shard_map/ppermute | solution.py:782
  49.4 23.9 %collective-permute-start.2 = (bf16[256,512]{1,0:T(8,128)(2,1)}, bf16[256,512]{1,0:T(8,128)(2,1)S(1)}, u32[]{:S(2)}, u32[]{:S(2)}) collective-permute-start(bf16[256,512]{1,0:T(8,128)(2,1)} %get-tuple-element.404), channel_id=1, source_target_pairs={{0,3},{1,2},{2,1},{3,0},{4,7},{5,6},{6,5},{7,4},{8,11},{9,10},{10,... | collective-permute-start | bytes 786440 | tf_op jit(solution)/shard_map/ppermute | solution.py:782
  53.4 44.9 %collective-permute-start.1 = (bf16[256,512]{1,0:T(8,128)(2,1)S(1)}, bf16[256,512]{1,0:T(8,128)(2,1)S(1)}, u32[]{:S(2)}, u32[]{:S(2)}) collective-permute-start(bf16[256,512]{1,0:T(8,128)(2,1)S(1)} %copy-done.29), channel_id=1, source_target_pairs={{0,2},{1,3},{2,0},{3,1},{4,6},{5,7},{6,4},{7,5},{8,10},{9,11},{10,... | collective-permute-start | bytes 786440 | tf_op jit(solution)/shard_map/ppermute | solution.py:782
  236.2 15.9 %collective-permute-start.9 = (bf16[256,6400]{1,0:T(8,128)(2,1)}, bf16[256,6400]{1,0:T(8,128)(2,1)}, u32[]{:S(2)}, u32[]{:S(2)}) collective-permute-start(bf16[256,6400]{1,0:T(8,128)(2,1)} %get-tuple-element.167), channel_id=1, source_target_pairs={{0,4},{4,0},{8,12},{12,8},{16,20},{20,16},{24,28},{28,24},{1,5},{5... | collective-permute-start | bytes 9830408 | tf_op jit(solution)/shard_map/ppermute | solution.py:782
  236.5 15.6 %collective-permute-start.10 = (bf16[256,4096]{1,0:T(8,128)(2,1)}, bf16[256,4096]{1,0:T(8,128)(2,1)}, u32[]{:S(2)}, u32[]{:S(2)}) collective-permute-start(bf16[256,4096]{1,0:T(8,128)(2,1)} %get-tuple-element.168), channel_id=1, source_target_pairs={{0,4},{4,0},{8,12},{12,8},{16,20},{20,16},{24,28},{28,24},{1,5},{5... | collective-permute-start | bytes 6291464 | tf_op jit(solution)/shard_map/ppermute | solution.py:782
  256.2 41.2 %collective-permute-start.13 = (bf16[64,6400]{1,0:T(8,128)(2,1)S(1)}, bf16[64,6400]{1,0:T(8,128)(2,1)}, u32[]{:S(2)}, u32[]{:S(2)}) collective-permute-start(bf16[64,6400]{1,0:T(8,128)(2,1)S(1)} %get-tuple-element.367), channel_id=1, source_target_pairs={{0,24},{4,28},{8,16},{12,20},{16,8},{20,12},{24,0},{28,4},{1,25},{... | collective-permute-start | bytes 2457608 | tf_op jit(solution)/shard_map/ppermute | solution.py:782
  257.6 39.9 %collective-permute-start.12 = (bf16[64,6400]{1,0:T(8,128)(2,1)S(1)}, bf16[64,6400]{1,0:T(8,128)(2,1)S(1)}, u32[]{:S(2)}, u32[]{:S(2)}) collective-permute-start(bf16[64,6400]{1,0:T(8,128)(2,1)S(1)} %get-tuple-element.368), channel_id=1, source_target_pairs={{0,16},{4,20},{8,24},{12,28},{16,0},{20,4},{24,8},{28,12},{1,17},{... | collective-permute-start | bytes 2457608 | tf_op jit(solution)/shard_map/ppermute | solution.py:782
  259.0 38.5 %collective-permute-start.11 = (bf16[64,6400]{1,0:T(8,128)(2,1)S(1)}, bf16[64,6400]{1,0:T(8,128)(2,1)S(1)}, u32[]{:S(2)}, u32[]{:S(2)}) collective-permute-start(bf16[64,6400]{1,0:T(8,128)(2,1)S(1)} %get-tuple-element.369), channel_id=1, source_target_pairs={{0,8},{4,12},{8,0},{12,4},{16,24},{20,28},{24,16},{28,20},{1,9},{5... | collective-permute-start | bytes 2457608 | tf_op jit(solution)/shard_map/ppermute | solution.py:782
  299.4 45.7 %collective-permute-start.20 = (bf16[256,6912]{1,0:T(8,128)(2,1)}, bf16[256,6912]{1,0:T(8,128)(2,1)S(1)}, u32[]{:S(2)}, u32[]{:S(2)}) collective-permute-start(bf16[256,6912]{1,0:T(8,128)(2,1)} %get-tuple-element.199), channel_id=1, source_target_pairs={{0,4},{4,0},{8,12},{12,8},{16,20},{20,16},{24,28},{28,24},{1,5},{5... | collective-permute-start | bytes 10616840 | tf_op jit(solution)/shard_map/ppermute | solution.py:782
  302.1 29.2 %collective-permute-start.16 = (bf16[16,6400]{1,0:T(8,128)(2,1)}, bf16[16,6400]{1,0:T(8,128)(2,1)}, u32[]{:S(2)}, u32[]{:S(2)}) collective-permute-start(bf16[16,6400]{1,0:T(8,128)(2,1)} %get-tuple-element.377), channel_id=1, source_target_pairs={{0,3},{1,2},{2,1},{3,0},{4,7},{5,6},{6,5},{7,4},{8,11},{9,10},{10,... | collective-permute-start | bytes 614408 | tf_op jit(solution)/shard_map/ppermute | solution.py:782
  303.9 30.4 %collective-permute-start.15 = (bf16[16,6400]{1,0:T(8,128)(2,1)}, bf16[16,6400]{1,0:T(8,128)(2,1)}, u32[]{:S(2)}, u32[]{:S(2)}) collective-permute-start(bf16[16,6400]{1,0:T(8,128)(2,1)} %get-tuple-element.378), channel_id=1, source_target_pairs={{0,2},{1,3},{2,0},{3,1},{4,6},{5,7},{6,4},{7,5},{8,10},{9,11},{10,... | collective-permute-start | bytes 614408 | tf_op jit(solution)/shard_map/ppermute | solution.py:782
  307.7 33.8 %collective-permute-start.19 = (bf16[64,4096]{1,0:T(8,128)(2,1)}, bf16[64,4096]{1,0:T(8,128)(2,1)}, u32[]{:S(2)}, u32[]{:S(2)}) collective-permute-start(bf16[64,4096]{1,0:T(8,128)(2,1)} %get-tuple-element.371), channel_id=1, source_target_pairs={{0,24},{4,28},{8,16},{12,20},{16,8},{20,12},{24,0},{28,4},{1,25},{... | collective-permute-start | bytes 1572872 | tf_op jit(solution)/shard_map/ppermute | solution.py:782
  309.1 32.4 %collective-permute-start.18 = (bf16[64,4096]{1,0:T(8,128)(2,1)}, bf16[64,4096]{1,0:T(8,128)(2,1)}, u32[]{:S(2)}, u32[]{:S(2)}) collective-permute-start(bf16[64,4096]{1,0:T(8,128)(2,1)} %get-tuple-element.372), channel_id=1, source_target_pairs={{0,16},{4,20},{8,24},{12,28},{16,0},{20,4},{24,8},{28,12},{1,17},{... | collective-permute-start | bytes 1572872 | tf_op jit(solution)/shard_map/ppermute | solution.py:782
  348.0 32.5 %collective-permute-start.23 = (bf16[16,4096]{1,0:T(8,128)(2,1)}, bf16[16,4096]{1,0:T(8,128)(2,1)}, u32[]{:S(2)}, u32[]{:S(2)}) collective-permute-start(bf16[16,4096]{1,0:T(8,128)(2,1)} %get-tuple-element.384), channel_id=1, source_target_pairs={{0,3},{1,2},{2,1},{3,0},{4,7},{5,6},{6,5},{7,4},{8,11},{9,10},{10,... | collective-permute-start | bytes 393224 | tf_op jit(solution)/shard_map/ppermute | solution.py:782
  350.0 31.8 %collective-permute-start.22 = (bf16[16,4096]{1,0:T(8,128)(2,1)}, bf16[16,4096]{1,0:T(8,128)(2,1)}, u32[]{:S(2)}, u32[]{:S(2)}) collective-permute-start(bf16[16,4096]{1,0:T(8,128)(2,1)} %get-tuple-element.385), channel_id=1, source_target_pairs={{0,2},{1,3},{2,0},{3,1},{4,6},{5,7},{6,4},{7,5},{8,10},{9,11},{10,... | collective-permute-start | bytes 393224 | tf_op jit(solution)/shard_map/ppermute | solution.py:782
  351.8 30.0 %collective-permute-start.21 = (bf16[16,4096]{1,0:T(8,128)(2,1)}, bf16[16,4096]{1,0:T(8,128)(2,1)}, u32[]{:S(2)}, u32[]{:S(2)}) collective-permute-start(bf16[16,4096]{1,0:T(8,128)(2,1)} %get-tuple-element.386), channel_id=1, source_target_pairs={{0,1},{1,0},{2,3},{3,2},{4,5},{5,4},{6,7},{7,6},{8,9},{9,8},{10,11... | collective-permute-start | bytes 393224 | tf_op jit(solution)/shard_map/ppermute | solution.py:782
  354.7 30.0 %collective-permute-start.26 = (bf16[64,6912]{1,0:T(8,128)(2,1)}, bf16[64,6912]{1,0:T(8,128)(2,1)}, u32[]{:S(2)}, u32[]{:S(2)}) collective-permute-start(bf16[64,6912]{1,0:T(8,128)(2,1)} %get-tuple-element.363), channel_id=1, source_target_pairs={{0,24},{4,28},{8,16},{12,20},{16,8},{20,12},{24,0},{28,4},{1,25},{... | collective-permute-start | bytes 2654216 | tf_op jit(solution)/shard_map/ppermute | solution.py:782
  356.2 38.1 %collective-permute-start.25 = (bf16[64,6912]{1,0:T(8,128)(2,1)}, bf16[64,6912]{1,0:T(8,128)(2,1)}, u32[]{:S(2)}, u32[]{:S(2)}) collective-permute-start(bf16[64,6912]{1,0:T(8,128)(2,1)} %get-tuple-element.364), channel_id=1, source_target_pairs={{0,16},{4,20},{8,24},{12,28},{16,0},{20,4},{24,8},{28,12},{1,17},{... | collective-permute-start | bytes 2654216 | tf_op jit(solution)/shard_map/ppermute | solution.py:782
  380.5 19.1 %collective-permute-start.24 = (bf16[64,6912]{1,0:T(8,128)(2,1)}, bf16[64,6912]{1,0:T(8,128)(2,1)S(1)}, u32[]{:S(2)}, u32[]{:S(2)}) collective-permute-start(bf16[64,6912]{1,0:T(8,128)(2,1)} %get-tuple-element.365), channel_id=1, source_target_pairs={{0,8},{4,12},{8,0},{12,4},{16,24},{20,28},{24,16},{28,20},{1,9},{5... | collective-permute-start | bytes 2654216 | tf_op jit(solution)/shard_map/ppermute | solution.py:782
  383.1 16.5 %collective-permute-start.27 = (bf16[256,2048]{1,0:T(8,128)(2,1)S(1)}, bf16[256,2048]{1,0:T(8,128)(2,1)S(1)}, u32[]{:S(2)}, u32[]{:S(2)}) collective-permute-start(bf16[256,2048]{1,0:T(8,128)(2,1)S(1)} %pad_maximum_fusion.2), channel_id=1, source_target_pairs={{0,4},{4,0},{8,12},{12,8},{16,20},{20,16},{24,28},{28,24},{1,5},{5... | collective-permute-start | bytes 3145736 | tf_op jit(solution)/shard_map/ppermute | solution.py:782
  399.7 23.9 %collective-permute-start.30 = (bf16[256,512]{1,0:T(8,128)(2,1)S(1)}, bf16[256,512]{1,0:T(8,128)(2,1)S(1)}, u32[]{:S(2)}, u32[]{:S(2)}) collective-permute-start(bf16[256,512]{1,0:T(8,128)(2,1)S(1)} %get-tuple-element.399), channel_id=1, source_target_pairs={{0,3},{1,2},{2,1},{3,0},{4,7},{5,6},{6,5},{7,4},{8,11},{9,10},{10,... | collective-permute-start | bytes 786440 | tf_op jit(solution)/shard_map/ppermute | solution.py:782
  401.8 26.1 %collective-permute-start.29 = (bf16[256,512]{1,0:T(8,128)(2,1)S(1)}, bf16[256,512]{1,0:T(8,128)(2,1)S(1)}, u32[]{:S(2)}, u32[]{:S(2)}) collective-permute-start(bf16[256,512]{1,0:T(8,128)(2,1)S(1)} %get-tuple-element.400), channel_id=1, source_target_pairs={{0,2},{1,3},{2,0},{3,1},{4,6},{5,7},{6,4},{7,5},{8,10},{9,11},{10,... | collective-permute-start | bytes 786440 | tf_op jit(solution)/shard_map/ppermute | solution.py:782
  402.3 31.5 %collective-permute-start.28 = (bf16[256,512]{1,0:T(8,128)(2,1)S(1)}, bf16[256,512]{1,0:T(8,128)(2,1)S(1)}, u32[]{:S(2)}, u32[]{:S(2)}) collective-permute-start(bf16[256,512]{1,0:T(8,128)(2,1)S(1)} %get-tuple-element.401), channel_id=1, source_target_pairs={{0,1},{1,0},{2,3},{3,2},{4,5},{5,4},{6,7},{7,6},{8,9},{9,8},{10,11... | collective-permute-start | bytes 786440 | tf_op jit(solution)/shard_map/ppermute | solution.py:782
  405.9 16.4 %collective-permute-start.39 = (bf16[16,6912]{1,0:T(8,128)(2,1)S(1)}, bf16[16,6912]{1,0:T(8,128)(2,1)S(1)}, u32[]{:S(2)}, u32[]{:S(2)}) collective-permute-start(bf16[16,6912]{1,0:T(8,128)(2,1)S(1)} %get-tuple-element.374), channel_id=1, source_target_pairs={{0,3},{1,2},{2,1},{3,0},{4,7},{5,6},{6,5},{7,4},{8,11},{9,10},{10,... | collective-permute-start | bytes 663560 | tf_op jit(solution)/shard_map/ppermute | solution.py:782
  408.4 33.7 %collective-permute-start.36 = (bf16[64,2048]{1,0:T(8,128)(2,1)S(1)}, bf16[64,2048]{1,0:T(8,128)(2,1)S(1)}, u32[]{:S(2)}, u32[]{:S(2)}) collective-permute-start(bf16[64,2048]{1,0:T(8,128)(2,1)S(1)} %get-tuple-element.380), channel_id=1, source_target_pairs={{0,24},{4,28},{8,16},{12,20},{16,8},{20,12},{24,0},{28,4},{1,25},{... | collective-permute-start | bytes 786440 | tf_op jit(solution)/shard_map/ppermute | solution.py:782
  422.3 19.8 %collective-permute-start.35 = (bf16[64,2048]{1,0:T(8,128)(2,1)S(1)}, bf16[64,2048]{1,0:T(8,128)(2,1)S(1)}, u32[]{:S(2)}, u32[]{:S(2)}) collective-permute-start(bf16[64,2048]{1,0:T(8,128)(2,1)S(1)} %get-tuple-element.381), channel_id=1, source_target_pairs={{0,16},{4,20},{8,24},{12,28},{16,0},{20,4},{24,8},{28,12},{1,17},{... | collective-permute-start | bytes 786440 | tf_op jit(solution)/shard_map/ppermute | solution.py:782
  423.6 18.5 %collective-permute-start.34 = (bf16[64,2048]{1,0:T(8,128)(2,1)S(1)}, bf16[64,2048]{1,0:T(8,128)(2,1)S(1)}, u32[]{:S(2)}, u32[]{:S(2)}) collective-permute-start(bf16[64,2048]{1,0:T(8,128)(2,1)S(1)} %get-tuple-element.382), channel_id=1, source_target_pairs={{0,8},{4,12},{8,0},{12,4},{16,24},{20,28},{24,16},{28,20},{1,9},{5... | collective-permute-start | bytes 786440 | tf_op jit(solution)/shard_map/ppermute | solution.py:782
  (49 other events, 843.7 us)
Sparse Core Ops, SparseCore 0:
  14.9 94.9 all-gather.2
  113.3 87.0 all-gather.4
